TPU v7x, 512 devices: a whole 4x4x16 slice. The times are simulated.
512 devices in a mesh: row: 32 (over z, x_lo), col: 16 (over y, x_hi, core).
Axes of the slice: x: 4 (x_hi: 2, x_lo: 2; x = x_hi * 2 + x_lo), y: 4, z: 16, core: 2. Of those that a mesh axis runs over, the one named last changes fastest.
Arguments:
- image: bfloat16 [256, 196608], P('row', 'col'), may hold values from -6 to 6
- cotangent: bfloat16 [256, 196608], P('row', 'col'), may hold values from -6 to 6
- qkv_weight: bfloat16 [192, 576], replicated, may hold values from -0.4375 to 0.4375
- qkv_bias: float32 [576], replicated, may hold values from -3 to 3
- proj_weight: bfloat16 [192, 192], replicated, may hold values from -0.4375 to 0.4375
- proj_bias: float32 [192], replicated, may hold values from -3 to 3
- norm_gain: float32 [192], replicated, may hold values from 0.1 to 1.9
- norm_bias: float32 [192], replicated, may hold values from -3 to 3
- bias_table: float32 [6, 225], replicated, may hold values from -4 to 304
Outputs:
- result: bfloat16 [256, 196608], P('row', 'col')
- grad_input: bfloat16 [256, 196608], P('row', 'col')
- grad_qkv_weight: float32 [192, 576], replicated
- grad_qkv_bias: float32 [576], replicated
- grad_proj_weight: float32 [192, 192], replicated
- grad_proj_bias: float32 [192], replicated
- grad_norm_gain: float32 [192], replicated
- grad_norm_bias: float32 [192], replicated
- grad_bias_table: float32 [6, 225], replicated
All inputs are finite; a program needn't handle non-finite values.
Results may differ from a plain program's by a relative error of at most 0.019.
Values may be sent and summed in bfloat16 or wider, within the bound.
A program may use at most 64 MiB of HBM per device.

v0:
```python
import jax
import jax.numpy as jnp
import numpy as np
from jax import lax
from jax.sharding import PartitionSpec as P

WIDTH = 192
HEADS = 6
HEAD_DIM = 32
WIN = 8
SHIFT = 4
RELS = 225


EPS = 1e-05
NEG = -1e30


def passed_along(value, axis, steps):
    count = lax.axis_size(axis)
    pairs = [(source, (source + steps) % count) for source in range(count)]
    return lax.ppermute(value, axis, pairs)


def product(spec, left, right):
    return jnp.einsum(spec, left, right, preferred_element_type=jnp.float32)


def offset_onehot():
    cells = np.arange(WIN * WIN)
    down = cells // WIN
    across = cells % WIN
    offset = (down[:, None] - down[None, :] + WIN - 1) * (2 * WIN - 1) + (
        across[:, None] - across[None, :] + WIN - 1
    )
    table = offset.reshape(-1)[:, None] == np.arange(RELS)[None, :]
    return jnp.asarray(table.astype(np.float32))


def to_windows(field, tile_rows, tile_cols):
    feats = field.shape[-1]
    field = field.reshape(tile_rows // WIN, WIN, tile_cols // WIN, WIN, feats)
    return field.transpose(0, 2, 1, 3, 4).reshape(-1, WIN * WIN, feats)


def from_windows(field, tile_rows, tile_cols):
    feats = field.shape[-1]
    field = field.reshape(tile_rows // WIN, tile_cols // WIN, WIN, WIN, feats)
    return field.transpose(0, 2, 1, 3, 4).reshape(tile_rows, tile_cols * feats)


def region(index, total):
    return (index >= total - WIN).astype(jnp.int32) + (index >= total - SHIFT).astype(jnp.int32)


def mask_for(row_start, col_start, tile_rows, tile_cols, total_rows, total_cols):
    grid_rows = row_start + jnp.arange(tile_rows, dtype=jnp.int32)
    grid_cols = col_start + jnp.arange(tile_cols, dtype=jnp.int32)
    label = region(grid_rows, total_rows)[:, None] * 3 + region(grid_cols, total_cols)[None, :]
    label = to_windows(label[:, :, None], tile_rows, tile_cols)[:, :, 0]
    return label[:, :, None] == label[:, None, :]


def roll_lead(stacked):
    arrived = passed_along(stacked[:, :SHIFT], "row", -1)
    stacked = jnp.concatenate([stacked[:, SHIFT:], arrived], 1)
    edge = SHIFT * WIDTH
    arrived = passed_along(stacked[:, :, :edge], "col", -1)
    return jnp.concatenate([stacked[:, :, edge:], arrived], 2)


def roll_trail(stacked):
    arrived = passed_along(stacked[:, -SHIFT:], "row", 1)
    stacked = jnp.concatenate([arrived, stacked[:, :-SHIFT]], 1)
    edge = SHIFT * WIDTH
    arrived = passed_along(stacked[:, :, -edge:], "col", 1)
    return jnp.concatenate([arrived, stacked[:, :, :-edge]], 2)


def forward(tile, params, allowed, tile_rows, tile_cols):
    qkv_weight, qkv_bias, proj_weight, proj_bias, norm_gain, norm_bias, bias_table = params
    tokens = to_windows(tile.reshape(tile_rows, tile_cols, WIDTH), tile_rows, tile_cols).astype(
        jnp.float32
    )
    win_count = tokens.shape[0]
    center = tokens - jnp.mean(tokens, -1, keepdims=True)
    inv_std = lax.rsqrt(jnp.mean(center * center, -1, keepdims=True) + EPS)
    normed = center * inv_std
    hidden = (normed * norm_gain + norm_bias).astype(jnp.bfloat16)
    packed = (product("wtc,cf->wtf", hidden, qkv_weight) + qkv_bias).astype(jnp.bfloat16)
    query_h = packed[..., :WIDTH].reshape(win_count, WIN * WIN, HEADS, HEAD_DIM)
    key_h = packed[..., WIDTH : 2 * WIDTH].reshape(win_count, WIN * WIN, HEADS, HEAD_DIM)
    value_h = packed[..., 2 * WIDTH :].reshape(win_count, WIN * WIN, HEADS, HEAD_DIM)
    rel = jnp.einsum("pr,hr->hp", offset_onehot(), bias_table, precision=lax.Precision.HIGHEST)
    rel = rel.reshape(HEADS, WIN * WIN, WIN * WIN)
    scores = product("wqhd,wkhd->whqk", query_h, key_h) * HEAD_DIM ** (-0.5) + rel[None]
    scores = jnp.where(allowed[:, None], scores, NEG)
    row_max = jnp.max(scores, -1, keepdims=True)
    expo = jnp.exp(scores - row_max)
    probs = expo / jnp.sum(expo, -1, keepdims=True)
    probs_b = probs.astype(jnp.bfloat16)
    attended = product("whqk,wkhd->wqhd", probs_b, value_h).astype(jnp.bfloat16)
    attended = attended.reshape(win_count, WIN * WIN, WIDTH)
    mixed = product("wtc,cf->wtf", attended, proj_weight) + proj_bias
    out = (tokens + mixed).astype(jnp.bfloat16)
    saved = (normed, inv_std, hidden, query_h, key_h, value_h, probs, probs_b, attended)
    return (from_windows(out, tile_rows, tile_cols), saved)


def backward(cot_tile, saved, params, tile_rows, tile_cols):
    qkv_weight, qkv_bias, proj_weight, proj_bias, norm_gain, norm_bias, bias_table = params
    normed, inv_std, hidden, query_h, key_h, value_h, probs, probs_b, attended = saved
    win_count = normed.shape[0]
    cot_win = to_windows(cot_tile.reshape(tile_rows, tile_cols, WIDTH), tile_rows, tile_cols)
    cot_float = cot_win.astype(jnp.float32)
    grad_proj_w = product("wtc,wtf->cf", attended, cot_win)
    grad_proj_b = jnp.sum(cot_float, (0, 1))
    d_attended = product("wtf,cf->wtc", cot_win, proj_weight).astype(jnp.bfloat16)
    d_attended = d_attended.reshape(win_count, WIN * WIN, HEADS, HEAD_DIM)
    d_probs = product("wqhd,wkhd->whqk", d_attended, value_h)
    d_value = product("whqk,wqhd->wkhd", probs_b, d_attended)
    d_scores = probs * (d_probs - jnp.sum(probs * d_probs, -1, keepdims=True))
    grad_table = jnp.einsum(
        "hp,pr->hr",
        jnp.sum(d_scores, 0).reshape(HEADS, WIN * WIN * WIN * WIN),
        offset_onehot(),
        precision=lax.Precision.HIGHEST,
    )
    d_scores_b = d_scores.astype(jnp.bfloat16)
    scale = HEAD_DIM ** (-0.5)
    d_query = product("whqk,wkhd->wqhd", d_scores_b, key_h) * scale
    d_key = product("whqk,wqhd->wkhd", d_scores_b, query_h) * scale
    shape_out = (win_count, WIN * WIN, WIDTH)
    d_packed = jnp.concatenate(
        [d_query.reshape(shape_out), d_key.reshape(shape_out), d_value.reshape(shape_out)], 2
    )
    d_packed_b = d_packed.astype(jnp.bfloat16)
    grad_qkv_w = product("wtc,wtf->cf", hidden, d_packed_b)
    grad_qkv_b = jnp.sum(d_packed, (0, 1))
    d_hidden = product("wtf,cf->wtc", d_packed_b, qkv_weight)
    grad_gain = jnp.sum(d_hidden * normed, (0, 1))
    grad_shift = jnp.sum(d_hidden, (0, 1))
    d_normed = d_hidden * norm_gain
    d_tokens = cot_float + inv_std * (
        d_normed
        - jnp.mean(d_normed, -1, keepdims=True)
        - normed * jnp.mean(d_normed * normed, -1, keepdims=True)
    )
    back = from_windows(d_tokens.astype(jnp.bfloat16), tile_rows, tile_cols)
    return (
        back,
        (grad_qkv_w, grad_qkv_b, grad_proj_w, grad_proj_b, grad_gain, grad_shift, grad_table),
    )


def shards(
    image, cotangent, qkv_weight, qkv_bias, proj_weight, proj_bias, norm_gain, norm_bias, bias_table
):
    params = (qkv_weight, qkv_bias, proj_weight, proj_bias, norm_gain, norm_bias, bias_table)
    tile_rows = image.shape[0]
    tile_cols = image.shape[1] // WIDTH
    total_rows = tile_rows * lax.axis_size("row")
    total_cols = tile_cols * lax.axis_size("col")
    allowed = mask_for(
        lax.axis_index("row") * tile_rows,
        lax.axis_index("col") * tile_cols,
        tile_rows,
        tile_cols,
        total_rows,
        total_cols,
    )
    moved_image = roll_lead(image[None])[0]
    out_tile, saved = forward(moved_image, params, allowed, tile_rows, tile_cols)
    result = roll_trail(out_tile[None])[0]
    moved_cot = roll_lead(cotangent[None])[0]
    back_tile, grads = backward(moved_cot, saved, params, tile_rows, tile_cols)
    grad_input = roll_trail(back_tile[None])[0]
    flat = jnp.concatenate([piece.reshape(-1) for piece in grads])
    total = lax.psum(flat, ("row", "col"))
    total = total * float(total_rows * total_cols) ** (-0.5)
    pieces = []
    offset = 0
    for piece in grads:
        count_here = piece.size
        pieces.append(total[offset : offset + count_here].reshape(piece.shape))
        offset = offset + count_here
    return (
        result,
        grad_input,
        pieces[0],
        pieces[1],
        pieces[2],
        pieces[3],
        pieces[4],
        pieces[5],
        pieces[6],
    )


def solution(mesh):
    in_specs = (P("row", "col"), P("row", "col"), P(), P(), P(), P(), P(), P(), P())
    out_specs = (P("row", "col"), P("row", "col"), P(), P(), P(), P(), P(), P(), P())
    return jax.shard_map(shards, mesh=mesh, in_specs=in_specs, out_specs=out_specs, check_vma=False)
```

profile of v0, /device:TPU:1, one launch (start us, length us, event | category | flops | bytes accessed | tf_op | source)
XLA Modules:
  0.0 539.8 jit_solution(3681478784735038246)
XLA Ops:
  7.2 1.2 fusion.47
  8.4 12.9 %collective-permute-start = (bf16[1,4,12288]{2,1,0:T(4,128)(2,1)S(1)}, bf16[1,4,12288]{2,1,0:T(4,128)(2,1)S(1)}, u32[]{:S(2)}, u32[]{:S(2)}) collective-permute-start(bf16[1,4,12288]{2,1,0:T(4,128)(2,1)S(1)} %get-tuple-element.28), channel_id=1, source_target_pairs={{0,496},{16,0},{32,16},{48,32},{64,48},{80,64},{96,80},{112,96},{1... | collective-permute-start | bytes 294920 | tf_op jit(solution)/shard_map/ppermute | solution.py:22
  21.3 1.1 fusion.45
  22.4 2.2 collective-permute-start.4
  24.8 5.8 %convolution_bitcast_fusion = f32[6,4096]{1,0:T(8,128)S(1)} fusion(f32[4096,225]{1,0:T(8,128)} %constant.45.clone, f32[6,225]{1,0:T(8,128)} %param.19), kind=kOutput, calls=%fused_computation.1 | convolution fusion | flops 66355200 | bytes 3790104 | tf_op jit(solution)/shard_map/pr,hr->hp/dot_general | solution.py:94
  31.7 3.1 collective-permute-start.1
  34.8 6.4 %collective-permute-start.5 = (bf16[1,8,768]{2,1,0:T(8,128)(2,1)S(1)}, bf16[1,8,768]{2,1,0:T(8,128)(2,1)S(1)}, u32[]{:S(2)}, u32[]{:S(2)}) collective-permute-start(bf16[1,8,768]{2,1,0:T(8,128)(2,1)S(1)} %pad_maximum_fusion.5), channel_id=1, source_target_pairs={{0,15},{1,0},{2,1},{3,2},{4,3},{5,4},{6,5},{7,6},{8,7},{9,8},{10,9... | collective-permute-start | bytes 36872 | tf_op jit(solution)/shard_map/ppermute | solution.py:22
  43.6 0.9 copy.79
  46.0 2.4 fusion.48
  48.4 2.2 multiply_reduce_fusion
  50.6 1.2 fusion.9
  53.3 1.4 fusion.14
  55.4 1.5 copy.93
  57.2 1.5 convolution_bitcast_fusion.1
  61.6 3.9 fusion.49
  66.0 7.7 %concatenate.39 = f32[149958]{0:T(1024)} concatenate(f32[110592]{0:T(1024)S(1)} %reshape.176, f32[576]{0:T(1024)S(1)} %fusion.7, f32[36864]{0:T(1024)S(1)} %reshape.177, f32[192]{0:T(256)S(1)} %convert_reduce_fusion, f32[192]{0:T(256)S(1)} %get-tuple-element.9, f32[192]{0:T(256)S(1)} %get-tuple-element.12, f32[1350]{0:T(1024)S(1)} %reshape.179), dimensions={0} | concatenate | bytes 1199664 | tf_op jit(solution)/shard_map/concatenate | solution.py:178
  74.5 2.2 collective-permute-start.6
  77.4 1.9 collective-permute-start.2
  79.3 2.6 collective-permute-done.6
  81.9 2.0 collective-permute-start.7
  84.8 4.6 collective-permute-start.3
  91.1 437.0 %all-reduce.2.cloned.1.call-done = f32[149958]{0:T(1024)} async-done(((f32[149958]{0:T(1024)}), f32[149958]{0:T(1024)}) %all-reduce.2.cloned.1.call-update) | async-done | bytes 599848 | tf_op jit(solution)/shard_map/psum | solution.py:179
  528.0 1.1 broadcast_multiply_fusion
  530.5 0.9 reshape.180
  (110 shorter events, 17.3 us)
Async XLA Ops:
  7.2 35.3 %copy-start = (bf16[192,576]{1,0:T(8,128)(2,1)S(1)}, bf16[192,576]{1,0:T(8,128)(2,1)}, u32[]{:S(2)}) copy-start(bf16[192,576]{1,0:T(8,128)(2,1)} %param.13) | copy-start | bytes 663556
  7.2 520.8 %all-reduce.2.cloned.1.call-start = ((), (), s32[]{:S(2)}) async-start(), calls=%async_computation | async-start | bytes 1204224 | tf_op jit(solution)/shard_map/psum | solution.py:179
  8.4 23.2 %collective-permute-start = (bf16[1,4,12288]{2,1,0:T(4,128)(2,1)S(1)}, bf16[1,4,12288]{2,1,0:T(4,128)(2,1)S(1)}, u32[]{:S(2)}, u32[]{:S(2)}) collective-permute-start(bf16[1,4,12288]{2,1,0:T(4,128)(2,1)S(1)} %get-tuple-element.28), channel_id=1, source_target_pairs={{0,496},{16,0},{32,16},{48,32},{64,48},{80,64},{96,80},{112,96},{1... | collective-permute-start | bytes 294920 | tf_op jit(solution)/shard_map/ppermute | solution.py:22
  22.4 12.4 %collective-permute-start.4 = (bf16[1,4,12288]{2,1,0:T(4,128)(2,1)S(1)}, bf16[1,4,12288]{2,1,0:T(4,128)(2,1)S(1)}, u32[]{:S(2)}, u32[]{:S(2)}) collective-permute-start(bf16[1,4,12288]{2,1,0:T(4,128)(2,1)S(1)} %get-tuple-element.24), channel_id=1, source_target_pairs={{0,496},{16,0},{32,16},{48,32},{64,48},{80,64},{96,80},{112,96},{1... | collective-permute-start | bytes 294920 | tf_op jit(solution)/shard_map/ppermute | solution.py:22
  31.7 9.9 %collective-permute-start.1 = (bf16[1,8,768]{2,1,0:T(8,128)(2,1)S(1)}, bf16[1,8,768]{2,1,0:T(8,128)(2,1)S(1)}, u32[]{:S(2)}, u32[]{:S(2)}) collective-permute-start(bf16[1,8,768]{2,1,0:T(8,128)(2,1)S(1)} %pad_maximum_fusion.7), channel_id=1, source_target_pairs={{0,15},{1,0},{2,1},{3,2},{4,3},{5,4},{6,5},{7,6},{8,7},{9,8},{10,9... | collective-permute-start | bytes 36872 | tf_op jit(solution)/shard_map/ppermute | solution.py:22
  34.8 9.7 %collective-permute-start.5 = (bf16[1,8,768]{2,1,0:T(8,128)(2,1)S(1)}, bf16[1,8,768]{2,1,0:T(8,128)(2,1)S(1)}, u32[]{:S(2)}, u32[]{:S(2)}) collective-permute-start(bf16[1,8,768]{2,1,0:T(8,128)(2,1)S(1)} %pad_maximum_fusion.5), channel_id=1, source_target_pairs={{0,15},{1,0},{2,1},{3,2},{4,3},{5,4},{6,5},{7,6},{8,7},{9,8},{10,9... | collective-permute-start | bytes 36872 | tf_op jit(solution)/shard_map/ppermute | solution.py:22
  41.4 1.0 copy-start.14
  43.1 1.7 copy-start.6
  48.4 2.2 copy-start.1
  48.4 2.2 copy-start.9
  51.8 1.4 copy-start.2
  51.8 1.5 copy-start.8
  55.4 1.8 copy-start.11
  55.4 1.8 copy-start.13
  55.4 1.8 copy-start.15
  55.4 1.8 copy-start.19
  58.7 1.4 copy-start.3
  58.7 1.5 copy-start.7
  60.1 1.3 copy-start.4
  73.7 3.0 copy-start.16
  74.5 7.5 %collective-permute-start.6 = (bf16[1,4,12288]{2,1,0:T(4,128)(2,1)S(1)}, bf16[1,4,12288]{2,1,0:T(4,128)(2,1)S(1)}, u32[]{:S(2)}, u32[]{:S(2)}) collective-permute-start(bf16[1,4,12288]{2,1,0:T(4,128)(2,1)S(1)} %get-tuple-element.21), channel_id=1, source_target_pairs={{0,16},{16,32},{32,48},{48,64},{64,80},{80,96},{96,112},{112,128},... | collective-permute-start | bytes 294920 | tf_op jit(solution)/shard_map/ppermute | solution.py:22
  77.4 7.5 %collective-permute-start.2 = (bf16[1,4,12288]{2,1,0:T(4,128)(2,1)S(1)}, bf16[1,4,12288]{2,1,0:T(4,128)(2,1)S(1)}, u32[]{:S(2)}, u32[]{:S(2)}) collective-permute-start(bf16[1,4,12288]{2,1,0:T(4,128)(2,1)S(1)} %get-tuple-element.25), channel_id=1, source_target_pairs={{0,16},{16,32},{32,48},{48,64},{64,80},{80,96},{96,112},{112,128},... | collective-permute-start | bytes 294920 | tf_op jit(solution)/shard_map/ppermute | solution.py:22
  81.9 7.5 %collective-permute-start.7 = (bf16[1,8,768]{2,1,0:T(8,128)(2,1)S(1)}, bf16[1,8,768]{2,1,0:T(8,128)(2,1)S(1)}, u32[]{:S(2)}, u32[]{:S(2)}) collective-permute-start(bf16[1,8,768]{2,1,0:T(8,128)(2,1)S(1)} %pad_maximum_fusion.4), channel_id=1, source_target_pairs={{0,1},{1,2},{2,3},{3,4},{4,5},{5,6},{6,7},{7,8},{8,9},{9,10},{10,1... | collective-permute-start | bytes 36872 | tf_op jit(solution)/shard_map/ppermute | solution.py:22
  84.8 5.4 %collective-permute-start.3 = (bf16[1,8,768]{2,1,0:T(8,128)(2,1)S(1)}, bf16[1,8,768]{2,1,0:T(8,128)(2,1)S(1)}, u32[]{:S(2)}, u32[]{:S(2)}) collective-permute-start(bf16[1,8,768]{2,1,0:T(8,128)(2,1)S(1)} %pad_maximum_fusion.6), channel_id=1, source_target_pairs={{0,1},{1,2},{2,3},{3,4},{4,5},{5,6},{6,7},{7,8},{8,9},{9,10},{10,1... | collective-permute-start | bytes 36872 | tf_op jit(solution)/shard_map/ppermute | solution.py:22
  (5 other events, 4.5 us)
Sparse Core Ops, SparseCore 0:
  73.8 454.1 all-reduce.1
where the time goes:
time: 540 us
  waiting for transfers between devices  441 us (82%)
  starting transfers between devices  35.4 us (7%)
  local copies, waits for them, and re-layouts  23.4 us (4%)
  matrix products  20.2 us (4%)
  between operations  14.7 us (3%)
  other arithmetic  5.48 us (1%)
    psum x1, waiting for transfers between devices, shards(): total = lax.psum(flat, ('row', 'col'))  437 us
    ppermute x8, starting transfers between devices, passed_along(): return lax.ppermute(value, axis, pairs)  35.4 us
  transfers between devices with their start and end apart: 9, of which 3 were waited for; matrix products, arithmetic and copies ran while one was open for 3% of the time, Pallas kernels for 0%

commit v1 on v0

--- a/solution.py
+++ b/solution.py
@@ -1,7 +1,11 @@
+import functools
+
 import jax
 import jax.numpy as jnp
 import numpy as np
 from jax import lax
+from jax.experimental import pallas as pl
+from jax.experimental.pallas import tpu as pltpu
 from jax.sharding import PartitionSpec as P
 
 WIDTH = 192
@@ -11,7 +15,8 @@
 SHIFT = 4
 RELS = 225
 
-
+MESH = pl.DeviceIdType.MESH
+ROW_AXIS, COL_AXIS = "row", "col"
 EPS = 1e-05
 NEG = -1e30
 
@@ -153,6 +158,184 @@
     )
 
 
+def reduce_kernel(n_row, n_col, tiles, per, scale, g_ref, o_ref, sbuf, rbuf, s2, r2, g2, fbuf,
+                  ss1, rs1, ss2, rs2, ss3, rs3, ss4, rs4):
+    my_r, my_c = lax.axis_index(ROW_AXIS), lax.axis_index(COL_AXIS)
+    lane_tiles = g_ref.shape[1] // 128
+    barrier = pltpu.get_barrier_semaphore()
+
+    def greet_col(k, _):
+        peer = lax.rem(my_c + k, n_col)
+        pl.semaphore_signal(barrier, inc=1, device_id=(my_r, peer), device_id_type=MESH)
+        return 0
+
+    def greet_row(k, _):
+        peer = lax.rem(my_r + k, n_row)
+        pl.semaphore_signal(barrier, inc=1, device_id=(peer, my_c), device_id_type=MESH)
+        return 0
+
+    lax.fori_loop(1, n_col, greet_col, 0)
+    lax.fori_loop(1, n_row, greet_row, 0)
+
+    for t in range(n_col * per):
+        if t < tiles:
+            rt, lt = t // lane_tiles, t % lane_tiles
+            tile = g_ref[rt * 16 : rt * 16 + 16, lt * 128 : lt * 128 + 128].astype(jnp.bfloat16)
+        else:
+            tile = jnp.zeros((16, 128), jnp.bfloat16)
+        sbuf[t // per, (t % per) * 16 : (t % per) * 16 + 16, :] = tile
+    pl.semaphore_wait(barrier, n_col - 1 + n_row - 1)
+
+    def scatter(peer, slot):
+        return pltpu.make_async_remote_copy(
+            src_ref=sbuf.at[peer], dst_ref=rbuf.at[slot], send_sem=ss1.at[peer],
+            recv_sem=rs1.at[slot], device_id=(my_r, peer), device_id_type=MESH)
+
+    def send1(k, _):
+        peer = lax.rem(my_c + k, n_col)
+        scatter(peer, my_c).start()
+        return 0
+
+    lax.fori_loop(1, n_col, send1, 0)
+    rbuf[my_c] = sbuf[my_c]
+
+    def recv1(k, _):
+        peer = lax.rem(my_c + k, n_col)
+        scatter(peer, peer).wait_recv()
+        return 0
+
+    lax.fori_loop(1, n_col, recv1, 0)
+    acc = rbuf[0].astype(jnp.float32)
+    for j in range(1, n_col):
+        acc = acc + rbuf[j].astype(jnp.float32)
+    acc = acc.astype(jnp.bfloat16)
+    for i in range(per):
+        s2[i] = acc[i * 16 : i * 16 + 16]
+
+    gap = n_row // per
+
+    def owner(i):
+        return lax.rem(i * gap + 2 * my_c, n_row)
+
+    def up(i):
+        return pltpu.make_async_remote_copy(
+            src_ref=s2.at[i], dst_ref=r2.at[my_r], send_sem=ss2.at[i],
+            recv_sem=rs2.at[my_r], device_id=(owner(i), my_c), device_id_type=MESH)
+
+    def up_from(peer):
+        return pltpu.make_async_remote_copy(
+            src_ref=s2.at[0], dst_ref=r2.at[peer], send_sem=ss2.at[0],
+            recv_sem=rs2.at[peer], device_id=(peer, my_c), device_id_type=MESH)
+
+    def down(i, peer):
+        return pltpu.make_async_remote_copy(
+            src_ref=g2.at[i], dst_ref=g2.at[i], send_sem=ss3.at[peer],
+            recv_sem=rs3.at[i], device_id=(peer, my_c), device_id_type=MESH)
+
+    for i in range(per):
+        @pl.when(owner(i) != my_r)
+        def _():
+            up(i).start()
+
+    for i in range(per):
+        @pl.when(owner(i) == my_r)
+        def _():
+            r2[my_r] = s2[i]
+
+            def recv2(k, _):
+                up_from(lax.rem(my_r + k, n_row)).wait_recv()
+                return 0
+
+            lax.fori_loop(1, n_row, recv2, 0)
+            total = r2[0].astype(jnp.float32)
+            for j in range(1, n_row):
+                total = total + r2[j].astype(jnp.float32)
+            g2[i] = total.astype(jnp.bfloat16)
+
+            def send3(k, _):
+                down(i, lax.rem(my_r + k, n_row)).start()
+                return 0
+
+            lax.fori_loop(1, n_row, send3, 0)
+
+    for i in range(per):
+        @pl.when(owner(i) != my_r)
+        def _():
+            down(i, my_r).wait_recv()
+
+    def gather(peer, slot):
+        return pltpu.make_async_remote_copy(
+            src_ref=g2, dst_ref=fbuf.at[slot], send_sem=ss4.at[peer],
+            recv_sem=rs4.at[slot], device_id=(my_r, peer), device_id_type=MESH)
+
+    def send4(k, _):
+        gather(lax.rem(my_c + k, n_col), my_c).start()
+        return 0
+
+    lax.fori_loop(1, n_col, send4, 0)
+    fbuf[my_c] = g2[...]
+
+    def recv4(k, _):
+        peer = lax.rem(my_c + k, n_col)
+        gather(peer, peer).wait_recv()
+        return 0
+
+    lax.fori_loop(1, n_col, recv4, 0)
+    for t in range(tiles):
+        rt, lt = t // lane_tiles, t % lane_tiles
+        o_ref[rt * 16 : rt * 16 + 16, lt * 128 : lt * 128 + 128] = (
+            fbuf[t // per, t % per].astype(jnp.float32) * scale)
+
+    def drain1(k, _):
+        peer = lax.rem(my_c + k, n_col)
+        scatter(peer, peer).wait_send()
+        gather(peer, peer).wait_send()
+        return 0
+
+    lax.fori_loop(1, n_col, drain1, 0)
+    for i in range(per):
+        @pl.when(owner(i) != my_r)
+        def _():
+            up(i).wait_send()
+
+        @pl.when(owner(i) == my_r)
+        def _():
+            def drain3(k, _):
+                down(i, lax.rem(my_r + k, n_row)).wait_send()
+                return 0
+
+            lax.fori_loop(1, n_row, drain3, 0)
+
+
+def all_reduce(g, n_row, n_col, scale):
+    tiles = (g.shape[0] // 16) * (g.shape[1] // 128)
+    per = -(-tiles // n_col)
+    return pl.pallas_call(
+        functools.partial(reduce_kernel, n_row, n_col, tiles, per, scale),
+        out_shape=jax.ShapeDtypeStruct(g.shape, jnp.float32),
+        in_specs=[pl.BlockSpec(memory_space=pltpu.VMEM)],
+        out_specs=pl.BlockSpec(memory_space=pltpu.VMEM),
+        scratch_shapes=[
+            pltpu.VMEM((n_col, per * 16, 128), jnp.bfloat16),
+            pltpu.VMEM((n_col, per * 16, 128), jnp.bfloat16),
+            pltpu.VMEM((per, 16, 128), jnp.bfloat16),
+            pltpu.VMEM((n_row, 16, 128), jnp.bfloat16),
+            pltpu.VMEM((per, 16, 128), jnp.bfloat16),
+            pltpu.VMEM((n_col, per, 16, 128), jnp.bfloat16),
+            pltpu.SemaphoreType.DMA((n_col,)),
+            pltpu.SemaphoreType.DMA((n_col,)),
+            pltpu.SemaphoreType.DMA((per,)),
+            pltpu.SemaphoreType.DMA((n_row,)),
+            pltpu.SemaphoreType.DMA((n_row,)),
+            pltpu.SemaphoreType.DMA((per,)),
+            pltpu.SemaphoreType.DMA((n_col,)),
+            pltpu.SemaphoreType.DMA((n_col,)),
+        ],
+        compiler_params=pltpu.CompilerParams(collective_id=1, has_side_effects=True,
+                                             vmem_limit_bytes=16 * 1024 * 1024),
+    )(g)
+
+
 def shards(
     image, cotangent, qkv_weight, qkv_bias, proj_weight, proj_bias, norm_gain, norm_bias, bias_table
 ):
@@ -175,15 +358,27 @@
     moved_cot = roll_lead(cotangent[None])[0]
     back_tile, grads = backward(moved_cot, saved, params, tile_rows, tile_cols)
     grad_input = roll_trail(back_tile[None])[0]
-    flat = jnp.concatenate([piece.reshape(-1) for piece in grads])
-    total = lax.psum(flat, ("row", "col"))
-    total = total * float(total_rows * total_cols) ** (-0.5)
-    pieces = []
-    offset = 0
-    for piece in grads:
-        count_here = piece.size
-        pieces.append(total[offset : offset + count_here].reshape(piece.shape))
-        offset = offset + count_here
+    grad_qkv_w, grad_qkv_b, grad_proj_w, grad_proj_b, grad_gain, grad_shift, grad_table = grads
+    wide = jnp.concatenate([grad_qkv_w, grad_proj_w], 1)
+    first = jnp.concatenate([grad_qkv_b, grad_proj_b])[None]
+    second = jnp.pad(jnp.concatenate([grad_gain, grad_shift])[None], ((0, 0), (0, 384)))
+    table = jnp.pad(grad_table, ((0, 8), (0, 768 - RELS)))
+    packed = jnp.concatenate([wide, first, second, table], 0)
+    total = all_reduce(
+        packed,
+        lax.axis_size("row"),
+        lax.axis_size("col"),
+        float(total_rows * total_cols) ** (-0.5),
+    )
+    pieces = [
+        total[:WIDTH, : 3 * WIDTH],
+        total[WIDTH, : 3 * WIDTH],
+        total[:WIDTH, 3 * WIDTH :],
+        total[WIDTH, 3 * WIDTH :],
+        total[WIDTH + 1, :WIDTH],
+        total[WIDTH + 1, WIDTH : 2 * WIDTH],
+        total[WIDTH + 2 : WIDTH + 2 + HEADS, :RELS],
+    ]
     return (
         result,
         grad_input,

time: 540 us -> 117 us (0.22)
  waiting for transfers between devices: 441 us -> 0.04 us
  Pallas kernels: 0 us -> 35.4 us
  between operations: 14.7 us -> 1.19 us
  local copies, waits for them, and re-layouts: 23.4 us -> 14.8 us
    psum x1 -> x0, waiting for transfers between devices: 437 us -> none  [shards(): total = lax.psum(flat, ('row', 'col'))]
    pallas_call x0 -> x1, Pallas kernels: none -> 35.4 us  [all_reduce(): pl.pallas_call(functools.partial(reduce_kernel, n_row, n_col, tiles, per,...]
    concatenate x1 -> x0, local copies, waits for them, and re-layouts: 7.68 us -> none  [shards(): flat = jnp.concatenate([piece.reshape(-1) for piece in grads])]
  transfers between devices with their start and end apart: 9 -> 8, of which waited for: 3 -> 0; matrix products, arithmetic and copies ran while one was open for 3% -> 12% of each run, Pallas kernels for 0% -> 0%
where the time goes in v1:
time: 117 us; the launch traced here: 116 us
  starting transfers between devices  40.1 us (34%)
  Pallas kernels  35.4 us (30%)
  matrix products  19.7 us (17%)
  local copies, waits for them, and re-layouts  14.8 us (13%)
  other arithmetic  4.59 us (4%)
  between operations  1.19 us (1%)
    ppermute x8, starting transfers between devices, passed_along(): return lax.ppermute(value, axis, pairs)  40.1 us
    pallas_call x1, Pallas kernels, all_reduce(): pl.pallas_call(functools.partial(reduce_kernel, n_row, n_col, tiles, per,...  35.4 us
    dot_general x11, matrix products, product(): return jnp.einsum(spec, left, right, preferred_element_type=jnp.float32)  8.1 us
    dot_general x1, matrix products, forward(): jnp.einsum('pr,hr->hp', offset_onehot(), bias_table, precision=lax.Precis...  5.8 us
    dot_general x1, matrix products, backward(): jnp.einsum('hp,pr->hr', jnp.sum(d_scores, 0).reshape(HEADS, WIN * WIN * W...  3.98 us
  transfers between devices with their start and end apart: 8, of which 0 were waited for; matrix products, arithmetic and copies ran while one was open for 12% of the time, Pallas kernels for 0%

profile of v1, /device:TPU:1, one launch (start us, length us, event | category | flops | bytes accessed | tf_op | source)
XLA Modules:
  0.0 115.9 jit_solution(2248532166794813101)
XLA Ops:
  0.7 1.1 fusion.48
  1.8 12.9 %collective-permute-start = (bf16[1,4,12288]{2,1,0:T(4,128)(2,1)S(1)}, bf16[1,4,12288]{2,1,0:T(4,128)(2,1)S(1)}, u32[]{:S(2)}, u32[]{:S(2)}) collective-permute-start(bf16[1,4,12288]{2,1,0:T(4,128)(2,1)S(1)} %get-tuple-element.28), channel_id=1, source_target_pairs={{0,496},{16,0},{32,16},{48,32},{64,48},{80,64},{96,80},{112,96},{1... | collective-permute-start | bytes 294920 | tf_op jit(solution)/shard_map/ppermute | solution.py:27
  14.7 1.1 fusion.46
  15.8 2.2 %collective-permute-start.4 = (bf16[1,4,12288]{2,1,0:T(4,128)(2,1)S(1)}, bf16[1,4,12288]{2,1,0:T(4,128)(2,1)S(1)}, u32[]{:S(2)}, u32[]{:S(2)}) collective-permute-start(bf16[1,4,12288]{2,1,0:T(4,128)(2,1)S(1)} %get-tuple-element.24), channel_id=1, source_target_pairs={{0,496},{16,0},{32,16},{48,32},{64,48},{80,64},{96,80},{112,96},{1... | collective-permute-start | bytes 294920 | tf_op jit(solution)/shard_map/ppermute | solution.py:27
  18.2 5.8 %convolution_bitcast_fusion = f32[6,4096]{1,0:T(8,128)S(1)} fusion(f32[4096,225]{1,0:T(8,128)} %constant.45.clone, f32[6,225]{1,0:T(8,128)} %param.19), kind=kOutput, calls=%fused_computation.1 | convolution fusion | flops 66355200 | bytes 3790104 | tf_op jit(solution)/shard_map/pr,hr->hp/dot_general | solution.py:99
  25.0 3.1 %collective-permute-start.1 = (bf16[1,8,768]{2,1,0:T(8,128)(2,1)S(1)}, bf16[1,8,768]{2,1,0:T(8,128)(2,1)S(1)}, u32[]{:S(2)}, u32[]{:S(2)}) collective-permute-start(bf16[1,8,768]{2,1,0:T(8,128)(2,1)S(1)} %pad_maximum_fusion.7), channel_id=1, source_target_pairs={{0,15},{1,0},{2,1},{3,2},{4,3},{5,4},{6,5},{7,6},{8,7},{9,8},{10,9... | collective-permute-start | bytes 36872 | tf_op jit(solution)/shard_map/ppermute | solution.py:27
  28.2 6.4 %collective-permute-start.5 = (bf16[1,8,768]{2,1,0:T(8,128)(2,1)S(1)}, bf16[1,8,768]{2,1,0:T(8,128)(2,1)S(1)}, u32[]{:S(2)}, u32[]{:S(2)}) collective-permute-start(bf16[1,8,768]{2,1,0:T(8,128)(2,1)S(1)} %pad_maximum_fusion.5), channel_id=1, source_target_pairs={{0,15},{1,0},{2,1},{3,2},{4,3},{5,4},{6,5},{7,6},{8,7},{9,8},{10,9... | collective-permute-start | bytes 36872 | tf_op jit(solution)/shard_map/ppermute | solution.py:27
  36.6 0.9 copy.81
  37.6 0.9 copy.79
  39.1 0.9 copy.87
  40.0 1.8 %fusion.49 = (f32[8,6,64]{2,1,0:T(8,128)S(1)}, f32[8,6,64,64]{2,3,1,0:T(8,128)S(1)}) fusion(bf16[8,64,6,32]{1,3,2,0:T(8,128)(2,1)S(1)} %bitcast.111, bf16[8,64,6,32]{1,3,2,0:T(8,128)(2,1)} %bitcast.113, f32[6,64,64]{1,2,0:T(8,128)S(1)} %copy.82, pred[8,64,64]{1,2,0:T(8,128)(4,1)} %broadcast_compare_fusion), kind=kOutput, calls=%fused_computation.100 | convolution fusion | flops 13566015 | bytes 1323008 | tf_op jit(solution)/shard_map/sub | solution.py:104
  41.8 2.2 %multiply_reduce_fusion = (f32[8,6,64]{2,1,0:T(8,128)S(1)}, f32[8,6,64,64]{2,3,1,0:T(8,128)S(1)}) fusion(f32[8,6,64,64]{2,3,1,0:T(8,128)S(1)} %get-tuple-element.30, f32[8,6,64]{2,1,0:T(8,128)S(1)} %get-tuple-element.29, bf16[8,64,6,32]{1,3,2,0:T(8,128)(2,1)} %bitcast.118, bf16[8,64,6,32]{1,3,2,0:T(8,128)(2,1)} %bitcast.116), kind=kOutput, calls=%fused_computation.4 | convolution fusion | flops 13169664 | bytes 1990656 | tf_op jit(solution)/shard_map/wqhd,wkhd->whqk/dot_general | solution.py:31
  46.5 1.4 %fusion.15 = f32[8,6,32,64]{3,2,1,0:T(8,128)} fusion(bf16[8,64,6,32]{1,3,2,0:T(8,128)(2,1)S(1)} %bitcast.119, f32[8,6,64,64]{2,3,1,0:T(8,128)S(1)} %copy-done.2, f32[8,6,64]{2,1,0:T(8,128)S(1)} %get-tuple-element.29), kind=kOutput, calls=%fused_computation.43 | convolution fusion | flops 12976128 | bytes 1388544 | tf_op jit(solution)/shard_map/whqk,wqhd->wkhd/dot_general | solution.py:31
  48.6 1.4 %copy.93 = f32[8,64,192]{2,1,0:T(8,128)S(1)} copy(f32[8,64,192]{1,2,0:T(8,128)} %bitcast.115) | data formatting | bytes 786432 | tf_op jit(solution)/shard_map/reshape | solution.py:140
  50.0 1.5 %convolution_bitcast_fusion.1 = f32[192,576]{1,0:T(8,128)} fusion(f32[192]{0:T(256)S(1)} %copy-done.13, f32[192]{0:T(256)S(1)} %copy-done.9, f32[8,64]{1,0:T(8,128)S(1)} %rsqrt.12, f32[8,64]{1,0:T(8,128)S(1)} %div.23, f32[1,8,8,8,192]{4,3,2,1,0:T(8,128)S(1)} %reshape.161, f32[8,64,192]{2,1,0:T(8,128)S(1)} %copy.93, f32[8,64,192]{2,1,0:T(8,128)S(1)} %copy.92, ...), kind=kOutput, calls=%fused_computation.15 | convolution fusion | flops 115507200 | bytes 2020864 | tf_op jit(solution)/shard_map/wtc,wtf->cf/dot_general | solution.py:31
  52.5 0.8 copy-done.3
  54.1 4.0 %fusion.50 = f32[6,225]{1,0:T(8,128)S(1)} fusion(f32[6,4096]{1,0:T(8,128)S(1)} %reshape.158, f32[4096,225]{1,0:T(8,128)} %constant.45.clone), kind=kOutput, calls=%fused_computation.101 | convolution fusion | flops 66355200 | bytes 3790104 | tf_op jit(solution)/shard_map/hp,pr->hr/dot_general | solution.py:128
  58.5 35.4 %shard_map.178 = f32[208,768]{1,0:T(8,128)S(1)} custom-call(f32[208,768]{1,0:T(8,128)S(1)} %select_maximum_fusion.g_ref), custom_call_target="tpu_custom_call" | custom-call | tf_op jit(solution)/shard_map/pallas_call | solution.py:313
  93.9 0.8 slice.97
  94.7 0.8 slice.99
  97.5 2.6 %collective-permute-start.6 = (bf16[1,4,12288]{2,1,0:T(4,128)(2,1)S(1)}, bf16[1,4,12288]{2,1,0:T(4,128)(2,1)S(1)}, u32[]{:S(2)}, u32[]{:S(2)}) collective-permute-start(bf16[1,4,12288]{2,1,0:T(4,128)(2,1)S(1)} %get-tuple-element.21), channel_id=1, source_target_pairs={{0,16},{16,32},{32,48},{48,64},{64,80},{80,96},{96,112},{112,128},... | collective-permute-start | bytes 294920 | tf_op jit(solution)/shard_map/ppermute | solution.py:27
  100.8 4.0 %collective-permute-start.2 = (bf16[1,4,12288]{2,1,0:T(4,128)(2,1)S(1)}, bf16[1,4,12288]{2,1,0:T(4,128)(2,1)S(1)}, u32[]{:S(2)}, u32[]{:S(2)}) collective-permute-start(bf16[1,4,12288]{2,1,0:T(4,128)(2,1)S(1)} %get-tuple-element.25), channel_id=1, source_target_pairs={{0,16},{16,32},{32,48},{48,64},{64,80},{80,96},{96,112},{112,128},... | collective-permute-start | bytes 294920 | tf_op jit(solution)/shard_map/ppermute | solution.py:27
  105.3 4.3 %collective-permute-start.7 = (bf16[1,8,768]{2,1,0:T(8,128)(2,1)S(1)}, bf16[1,8,768]{2,1,0:T(8,128)(2,1)S(1)}, u32[]{:S(2)}, u32[]{:S(2)}) collective-permute-start(bf16[1,8,768]{2,1,0:T(8,128)(2,1)S(1)} %pad_maximum_fusion.4), channel_id=1, source_target_pairs={{0,1},{1,2},{2,3},{3,4},{4,5},{5,6},{6,7},{7,8},{8,9},{9,10},{10,1... | collective-permute-start | bytes 36872 | tf_op jit(solution)/shard_map/ppermute | solution.py:27
  109.7 4.6 %collective-permute-start.3 = (bf16[1,8,768]{2,1,0:T(8,128)(2,1)S(1)}, bf16[1,8,768]{2,1,0:T(8,128)(2,1)S(1)}, u32[]{:S(2)}, u32[]{:S(2)}) collective-permute-start(bf16[1,8,768]{2,1,0:T(8,128)(2,1)S(1)} %pad_maximum_fusion.6), channel_id=1, source_target_pairs={{0,1},{1,2},{2,3},{3,4},{4,5},{5,6},{6,7},{7,8},{8,9},{9,10},{10,1... | collective-permute-start | bytes 36872 | tf_op jit(solution)/shard_map/ppermute | solution.py:27
  (93 shorter events, 13.6 us)
Async XLA Ops:
  0.6 35.1 %copy-start = (bf16[192,576]{1,0:T(8,128)(2,1)S(1)}, bf16[192,576]{1,0:T(8,128)(2,1)}, u32[]{:S(2)}) copy-start(bf16[192,576]{1,0:T(8,128)(2,1)} %param.13) | copy-start | bytes 663556
  1.8 23.2 %collective-permute-start = (bf16[1,4,12288]{2,1,0:T(4,128)(2,1)S(1)}, bf16[1,4,12288]{2,1,0:T(4,128)(2,1)S(1)}, u32[]{:S(2)}, u32[]{:S(2)}) collective-permute-start(bf16[1,4,12288]{2,1,0:T(4,128)(2,1)S(1)} %get-tuple-element.28), channel_id=1, source_target_pairs={{0,496},{16,0},{32,16},{48,32},{64,48},{80,64},{96,80},{112,96},{1... | collective-permute-start | bytes 294920 | tf_op jit(solution)/shard_map/ppermute | solution.py:27
  15.8 12.3 %collective-permute-start.4 = (bf16[1,4,12288]{2,1,0:T(4,128)(2,1)S(1)}, bf16[1,4,12288]{2,1,0:T(4,128)(2,1)S(1)}, u32[]{:S(2)}, u32[]{:S(2)}) collective-permute-start(bf16[1,4,12288]{2,1,0:T(4,128)(2,1)S(1)} %get-tuple-element.24), channel_id=1, source_target_pairs={{0,496},{16,0},{32,16},{48,32},{64,48},{80,64},{96,80},{112,96},{1... | collective-permute-start | bytes 294920 | tf_op jit(solution)/shard_map/ppermute | solution.py:27
  25.0 9.9 %collective-permute-start.1 = (bf16[1,8,768]{2,1,0:T(8,128)(2,1)S(1)}, bf16[1,8,768]{2,1,0:T(8,128)(2,1)S(1)}, u32[]{:S(2)}, u32[]{:S(2)}) collective-permute-start(bf16[1,8,768]{2,1,0:T(8,128)(2,1)S(1)} %pad_maximum_fusion.7), channel_id=1, source_target_pairs={{0,15},{1,0},{2,1},{3,2},{4,3},{5,4},{6,5},{7,6},{8,7},{9,8},{10,9... | collective-permute-start | bytes 36872 | tf_op jit(solution)/shard_map/ppermute | solution.py:27
  28.2 10.3 %collective-permute-start.5 = (bf16[1,8,768]{2,1,0:T(8,128)(2,1)S(1)}, bf16[1,8,768]{2,1,0:T(8,128)(2,1)S(1)}, u32[]{:S(2)}, u32[]{:S(2)}) collective-permute-start(bf16[1,8,768]{2,1,0:T(8,128)(2,1)S(1)} %pad_maximum_fusion.5), channel_id=1, source_target_pairs={{0,15},{1,0},{2,1},{3,2},{4,3},{5,4},{6,5},{7,6},{8,7},{9,8},{10,9... | collective-permute-start | bytes 36872 | tf_op jit(solution)/shard_map/ppermute | solution.py:27
  34.7 1.0 copy-start.9
  34.7 1.0 copy-start.12
  34.7 1.0 copy-start.13
  36.4 2.4 %copy-start.6 = (bf16[192,192]{1,0:T(8,128)(2,1)S(1)}, bf16[192,192]{1,0:T(8,128)(2,1)}, u32[]{:S(2)}) copy-start(bf16[192,192]{1,0:T(8,128)(2,1)} %param.15) | copy-start | bytes 221188
  41.8 2.2 %copy-start.1 = (f32[8,6,64,64]{2,3,1,0:T(8,128)}, f32[8,6,64,64]{2,3,1,0:T(8,128)S(1)}, u32[]{:S(2)}) copy-start(f32[8,6,64,64]{2,3,1,0:T(8,128)S(1)} %get-tuple-element.30) | copy-start | bytes 2359300
  44.1 1.0 copy-start.4
  45.1 1.4 %copy-start.2 = (f32[8,6,64,64]{2,3,1,0:T(8,128)S(1)}, f32[8,6,64,64]{2,3,1,0:T(8,128)}, u32[]{:S(2)}) copy-start(f32[8,6,64,64]{2,3,1,0:T(8,128)} %copy-done.1) | copy-start | bytes 2359300
  45.1 1.5 %copy-start.8 = (bf16[8,64,192]{1,2,0:T(8,128)(2,1)S(1)}, bf16[8,64,192]{1,2,0:T(8,128)(2,1)}, u32[]{:S(2)}) copy-start(bf16[8,64,192]{1,2,0:T(8,128)(2,1)} %copy.87) | copy-start | bytes 589828
  51.9 1.4 %copy-start.3 = (f32[8,6,64,64]{2,3,1,0:T(8,128)S(1)}, f32[8,6,64,64]{2,3,1,0:T(8,128)}, u32[]{:S(2)}) copy-start(f32[8,6,64,64]{2,3,1,0:T(8,128)} %copy-done.1) | copy-start | bytes 2359300
  51.9 1.5 %copy-start.7 = (bf16[8,64,192]{1,2,0:T(8,128)(2,1)S(1)}, bf16[8,64,192]{1,2,0:T(8,128)(2,1)}, u32[]{:S(2)}) copy-start(bf16[8,64,192]{1,2,0:T(8,128)(2,1)} %copy.79) | copy-start | bytes 589828
  54.1 4.3 %copy-start.5 = (f32[192,576]{1,0:T(8,128)S(1)}, f32[192,576]{1,0:T(8,128)}, u32[]{:S(2)}) copy-start(f32[192,576]{1,0:T(8,128)} %convolution_bitcast_fusion.1) | copy-start | bytes 1327108
  58.5 38.3 %copy-start.10 = (f32[192]{0:T(256)S(1)}, f32[192]{0:T(256)}, u32[]{:S(2)}) copy-start(f32[192]{0:T(256)} %param.17) | copy-start | bytes 2308
  95.5 4.6 %copy-start.11 = (f32[192]{0:T(256)S(1)}, f32[192]{0:T(256)}, u32[]{:S(2)}) copy-start(f32[192]{0:T(256)} %param.16) | copy-start | bytes 2308
  97.5 7.8 %collective-permute-start.6 = (bf16[1,4,12288]{2,1,0:T(4,128)(2,1)S(1)}, bf16[1,4,12288]{2,1,0:T(4,128)(2,1)S(1)}, u32[]{:S(2)}, u32[]{:S(2)}) collective-permute-start(bf16[1,4,12288]{2,1,0:T(4,128)(2,1)S(1)} %get-tuple-element.21), channel_id=1, source_target_pairs={{0,16},{16,32},{32,48},{48,64},{64,80},{80,96},{96,112},{112,128},... | collective-permute-start | bytes 294920 | tf_op jit(solution)/shard_map/ppermute | solution.py:27
  100.8 8.9 %collective-permute-start.2 = (bf16[1,4,12288]{2,1,0:T(4,128)(2,1)S(1)}, bf16[1,4,12288]{2,1,0:T(4,128)(2,1)S(1)}, u32[]{:S(2)}, u32[]{:S(2)}) collective-permute-start(bf16[1,4,12288]{2,1,0:T(4,128)(2,1)S(1)} %get-tuple-element.25), channel_id=1, source_target_pairs={{0,16},{16,32},{32,48},{48,64},{64,80},{80,96},{96,112},{112,128},... | collective-permute-start | bytes 294920 | tf_op jit(solution)/shard_map/ppermute | solution.py:27
  105.3 9.0 %collective-permute-start.7 = (bf16[1,8,768]{2,1,0:T(8,128)(2,1)S(1)}, bf16[1,8,768]{2,1,0:T(8,128)(2,1)S(1)}, u32[]{:S(2)}, u32[]{:S(2)}) collective-permute-start(bf16[1,8,768]{2,1,0:T(8,128)(2,1)S(1)} %pad_maximum_fusion.4), channel_id=1, source_target_pairs={{0,1},{1,2},{2,3},{3,4},{4,5},{5,6},{6,7},{7,8},{8,9},{9,10},{10,1... | collective-permute-start | bytes 36872 | tf_op jit(solution)/shard_map/ppermute | solution.py:27
  109.7 5.4 %collective-permute-start.3 = (bf16[1,8,768]{2,1,0:T(8,128)(2,1)S(1)}, bf16[1,8,768]{2,1,0:T(8,128)(2,1)S(1)}, u32[]{:S(2)}, u32[]{:S(2)}) collective-permute-start(bf16[1,8,768]{2,1,0:T(8,128)(2,1)S(1)} %pad_maximum_fusion.6), channel_id=1, source_target_pairs={{0,1},{1,2},{2,3},{3,4},{4,5},{5,6},{6,7},{7,8},{8,9},{9,10},{10,1... | collective-permute-start | bytes 36872 | tf_op jit(solution)/shard_map/ppermute | solution.py:27

commit v2 on v1

v2 whole, which is shorter than its diff:
```python
import functools

import jax
import jax.numpy as jnp
from jax import lax
from jax.experimental import pallas as pl
from jax.experimental.pallas import tpu as pltpu
from jax.sharding import PartitionSpec as P

WIDTH = 192
HEADS = 6
HEAD_DIM = 32
WIN = 8
CELLS = WIN * WIN
SHIFT = 4
RELS = 225
EPS = 1e-05
NEG = -1e30
TILE_COLS = 64
LANES = TILE_COLS * WIDTH
HALF = LANES // 2
EDGE = SHIFT * WIDTH
WINDOWS = TILE_COLS // WIN
SPAN = WIN * WIDTH
TOKENS_HERE = WINDOWS * CELLS
SCALE = HEAD_DIM**-0.5
GROUPS = ((0, 4), (4, 2))
TILES = 78
UNROLL = 2

MESH = pl.DeviceIdType.MESH
F32 = jnp.float32
BF16 = jnp.bfloat16


def dot(a, b, ca=1, cb=0):
    return lax.dot_general(a, b, (((ca,), (cb,)), ((), ())), preferred_element_type=F32)


def iota(shape, dim):
    return lax.broadcasted_iota(jnp.int32, shape, dim)


def upper(shape):
    return iota(shape, 0) < SHIFT


def pack_rows(field):
    back = pltpu.roll(field[:, HALF:], SHIFT, 0)
    return jnp.where(upper((WIN, HALF)), field[:, :HALF], back)


def merge_rows(packed, field):
    low = jnp.where(upper((WIN, HALF)), packed, field[:, :HALF])
    high = jnp.where(upper((WIN, HALF)), pltpu.roll(packed, SHIFT, 0), field[:, HALF:])
    return low, high


def split_tokens(strip):
    left = iota((WIN, 128), 1) < 64
    first, second = [], []
    for j in range(WIN // 2):
        v = [strip[:, (3 * j + i) * 128 : (3 * j + i + 1) * 128] for i in range(3)]
        r1, r2 = pltpu.roll(v[1], 64, 1), pltpu.roll(v[2], 64, 1)
        first += [v[0], jnp.where(left, r1, r2)]
        second += [v[1], r2]
    return jnp.concatenate(first, 0), jnp.concatenate(second, 0)


def join_tokens(first, second):
    left = iota((WIN, 128), 1) < 64
    out = []
    for j in range(WIN // 2):
        e = slice(16 * j, 16 * j + 8)
        o = slice(16 * j + 8, 16 * j + 16)
        swapped = pltpu.roll(first[o], 64, 1)
        out.append(first[e])
        out.append(jnp.where(left, second[e], swapped))
        out.append(jnp.where(left, swapped, pltpu.roll(second[o], 64, 1)))
    return jnp.concatenate(out, 1)


def build_bias(table_ref, onehot, padded, diag, bias, last_row, last_col):
    padded[...] = jnp.zeros((8, 256), F32)
    padded[0:HEADS, 0:RELS] = table_ref[...]
    table = padded[...]
    hi = table.astype(BF16)
    rest = table - hi.astype(F32)
    mid = rest.astype(BF16)
    low = (rest - mid.astype(F32)).astype(BF16)
    lane = iota((1, 128), 1)
    a_q = (lane + SHIFT) % WIN
    for a in range(WIN):
        target = (a_q - (a + SHIFT) % WIN + WIN - 1) * (2 * WIN - 1) + lane // WIN
        target = jnp.where(lane < 120, target, -1)
        hot = jnp.where(iota((256, 128), 0) == target, 1.0, 0.0).astype(BF16)
        onehot[a] = hot
        rows = dot(hi, hot) + dot(mid, hot) + dot(low, hot)
        for h in range(HEADS):
            diag[h, a : a + 1, :] = rows[h : h + 1, :]
    sub = iota((WIN, 128), 0)
    lanes = iota((WIN, 128), 1)
    row_cut = jnp.where((sub < SHIFT) != (lanes % WIN < SHIFT), NEG, 0.0) * last_row
    right = lanes % 64 // WIN >= SHIFT
    for b in range(WIN):
        col_cut = jnp.where(right != (b >= SHIFT), NEG, 0.0) * last_col
        for pair in range(HEADS // 2):
            shift = (WIN - 1 - b) * WIN
            even = pltpu.roll(diag[2 * pair], (128 - shift) % 128, 1)
            odd = pltpu.roll(diag[2 * pair + 1], (192 - shift) % 128, 1)
            block = jnp.where(lanes < 64, even, odd) + row_cut
            where = (slice(b * WIN, b * WIN + WIN), slice(pair * 128, pair * 128 + 128))
            bias[(0,) + where] = block
            bias[(1,) + where] = block + col_cut


def table_grad(total, onehot, diag):
    lanes = iota((WIN, 128), 1)
    for h in range(HEADS):
        mine = (lanes < 64) == (h % 2 == 0)
        acc = jnp.zeros((WIN, 128), F32)
        for b in range(WIN):
            block = total[b * WIN : b * WIN + WIN, h // 2 * 128 : h // 2 * 128 + 128]
            block = jnp.where(mine, block, 0.0)
            acc = acc + pltpu.roll(block, ((WIN - 1 - b) * WIN + h % 2 * 64) % 128, 1)
        diag[h] = acc
    flat = jnp.concatenate([diag[h] for h in range(HEADS)], 0)
    hi = flat.astype(BF16)
    low = (flat - hi.astype(F32)).astype(BF16)
    sub = iota((HEADS * WIN, 256), 0) % WIN
    acc = jnp.zeros((HEADS * WIN, 256), F32)
    for a in range(WIN):
        part = dot(hi, onehot[a], 1, 1) + dot(low, onehot[a], 1, 1)
        acc = acc + jnp.where(sub == a, part, 0.0)
    return [
        jnp.sum(acc[h * WIN : h * WIN + WIN], 0, keepdims=True) for h in range(HEADS)
    ]


def masked_heads(x, group):
    start, count = group
    lane = iota((CELLS, count * HEAD_DIM), 1) // HEAD_DIM
    wide = x[:, start * HEAD_DIM : (start + count) * HEAD_DIM]
    zero = jnp.zeros_like(wide)
    return jnp.concatenate([jnp.where(lane == h, wide, zero) for h in range(count)], 0)


def own_heads(x, count):
    lane = iota((CELLS, count * HEAD_DIM), 1) // HEAD_DIM
    out = x[(count - 1) * CELLS : count * CELLS]
    for h in range(count - 1):
        out = jnp.where(lane == h, x[h * CELLS : (h + 1) * CELLS], out)
    return out


def window_step(w, qs, ks, vs, das, bias, att, dq, dk, dv, gsum, last):
    rows = pl.ds(pl.multiple_of(w * CELLS, CELLS), CELLS)
    q, k, v, da = qs[rows, :], ks[rows, :], vs[rows, :], das[rows, :]
    for start, count in GROUPS:
        ch = slice(start * HEAD_DIM, (start + count) * HEAD_DIM)
        lanes = slice(start * CELLS, (start + count) * CELLS)
        qm = masked_heads(q, (start, count))
        dam = masked_heads(da, (start, count))
        s = dot(k[:, ch], qm, 1, 1) * SCALE + bias[last, :, lanes]
        e = jnp.exp(s - jnp.max(s, 0, keepdims=True))
        p = e * (1.0 / jnp.sum(e, 0, keepdims=True))
        dp = dot(v[:, ch], dam, 1, 1)
        ds = p * (dp - jnp.sum(p * dp, 0, keepdims=True))
        gsum[:, lanes] += ds
        pb, dsb = p.astype(BF16), ds.astype(BF16)
        dv[rows, ch] = dot(pb, dam)
        dk[rows, ch] = dot(dsb, qm) * SCALE
        att[rows, ch] = own_heads(dot(pb, v[:, ch], 0, 0), count).astype(BF16)
        dq[rows, ch] = own_heads(dot(dsb, k[:, ch], 0, 0), count) * SCALE


def block_kernel(n_row, n_col, per, grad_scale, *refs):
    (img, cot, wqkv, bqkv, wproj, bproj, gain_ref, shift_ref, table_ref,
     res, gin, g_qkv_w, g_qkv_b, g_proj_w, g_proj_b, g_gain, g_shift, g_table,
     irow, icol, hrow, hcol, hdiag, orow, ocol, rrow, rcol, rdiag,
     field, cfield, xs, cs, norm, hid, qs, ks, vs, das, att, dq, dk, dv, gsum,
     bias, onehot, padded, diag, gs, sbuf, rbuf, s2, r2, g2, fbuf,
     hs, hr, ss1, rs1, ss2, rs2, ss3, rs3, ss4, rs4) = refs
    my_r, my_c = lax.axis_index("row"), lax.axis_index("col")
    above, below = lax.rem(my_r + n_row - 1, n_row), lax.rem(my_r + 1, n_row)
    left, right = lax.rem(my_c + n_col - 1, n_col), lax.rem(my_c + 1, n_col)
    barrier = pltpu.get_barrier_semaphore()

    def greet(r, c):
        pl.semaphore_signal(barrier, inc=1, device_id=(r, c), device_id_type=MESH)

    greet(above, left)
    greet(below, right)

    def greet_col(k, _):
        greet(my_r, lax.rem(my_c + k, n_col))
        return 0

    def greet_row(k, _):
        greet(lax.rem(my_r + k, n_row), my_c)
        return 0

    lax.fori_loop(1, n_row, greet_row, 0)
    lax.fori_loop(1, n_col, greet_col, 0)

    def remote(src, dst, i, r, c):
        return pltpu.make_async_remote_copy(
            src_ref=src, dst_ref=dst, send_sem=hs.at[i], recv_sem=hr.at[i],
            device_id=(r, c), device_id_type=MESH)

    lead = (remote(irow, hrow, 0, above, my_c), remote(icol, hcol, 1, my_r, left),
            remote(icol, hdiag, 2, above, left))
    trail = (remote(orow, rrow, 3, below, my_c), remote(ocol, rcol, 4, my_r, right),
             remote(ocol, rdiag, 5, below, right))

    for i, src in enumerate((img, cot)):
        half = slice(i * WIN, i * WIN + WIN)
        tile = src[...].astype(F32)
        irow[half, :] = pack_rows(tile).astype(BF16)
        icol[half, :] = tile[:, :EDGE].astype(BF16)
    pl.semaphore_wait(barrier, n_row - 1 + n_col - 1 + 2)
    for copy in lead:
        copy.start()

    last_row = (my_r == n_row - 1).astype(F32)
    last_col = (my_c == n_col - 1).astype(F32)
    build_bias(table_ref, onehot, padded, diag, bias, last_row, last_col)
    gsum[...] = jnp.zeros_like(gsum)
    gs[WIDTH:, :] = jnp.zeros((16, 4 * WIDTH), F32)
    weights = [wqkv[:, i * WIDTH : (i + 1) * WIDTH] for i in range(3)]
    biases = [bqkv[:, i * WIDTH : (i + 1) * WIDTH] for i in range(3)]

    for copy in lead:
        copy.wait_recv()
    for i, (src, dst) in enumerate(((img, field), (cot, cfield))):
        half = slice(i * WIN, i * WIN + WIN)
        low, high = merge_rows(hrow[half, :].astype(F32), src[...].astype(F32))
        dst[:, :HALF] = low
        dst[:, HALF:LANES] = high
        dst[:, LANES:] = jnp.where(
            upper((WIN, EDGE)), hdiag[half, :].astype(F32), hcol[half, :].astype(F32))

    def tokens_of(w, _):
        lanes = pl.ds(pl.multiple_of(EDGE + w * SPAN, 128), SPAN)
        rows = pl.ds(pl.multiple_of(w * CELLS, CELLS), CELLS)
        for src, dst in ((field, xs), (cfield, cs)):
            first, second = split_tokens(src[:, lanes])
            dst[rows, 0:128] = first
            dst[rows, 128:WIDTH] = second[:, : WIDTH - 128]
        return 0

    lax.fori_loop(0, WINDOWS, tokens_of, 0)
    x = xs[...]
    center = x - jnp.mean(x, 1, keepdims=True)
    inv_std = lax.rsqrt(jnp.mean(center * center, 1, keepdims=True) + EPS)
    normed = center * inv_std
    norm[...] = normed
    gain = gain_ref[...]
    hidden = (normed * gain + shift_ref[...]).astype(BF16)
    hid[...] = hidden
    for dst, weight, add in zip((qs, ks, vs), weights, biases):
        dst[...] = (dot(hidden, weight) + add).astype(BF16)
    cot_b = cs[...].astype(BF16)
    das[...] = dot(cot_b, wproj[...], 1, 1).astype(BF16)

    def windows(i, _):
        for u in range(UNROLL):
            w = i * UNROLL + u
            last = (w == WINDOWS - 1).astype(jnp.int32)
            window_step(w, qs, ks, vs, das, bias, att, dq, dk, dv, gsum, last)
        return 0

    lax.fori_loop(0, WINDOWS // UNROLL, windows, 0)

    d_hidden = jnp.zeros((TOKENS_HERE, WIDTH), F32)
    hidden_t = hid[...].T
    for i, (part, weight) in enumerate(zip((dq, dk, dv), weights)):
        part_f = part[...]
        part_b = part_f.astype(BF16)
        lanes = slice(i * WIDTH, (i + 1) * WIDTH)
        gs[WIDTH : WIDTH + 1, lanes] = jnp.sum(part_f, 0, keepdims=True)
        gs[0:WIDTH, lanes] = dot(hidden_t, part_b)
        d_hidden = d_hidden + dot(part_b, weight, 1, 1)
    cot_b = cs[...].astype(BF16)
    gs[0:WIDTH, 3 * WIDTH :] = dot(att[...], cot_b, 0, 0)
    gs[WIDTH : WIDTH + 1, 3 * WIDTH :] = jnp.sum(cs[...], 0, keepdims=True)
    normed = norm[...]
    gs[WIDTH + 1 : WIDTH + 2, 0:WIDTH] = jnp.sum(d_hidden * normed, 0, keepdims=True)
    gs[WIDTH + 1 : WIDTH + 2, WIDTH : 2 * WIDTH] = jnp.sum(d_hidden, 0, keepdims=True)
    for h, line in enumerate(table_grad(gsum[...], onehot, diag)):
        gs[WIDTH + 2 + h : WIDTH + 3 + h, 0:256] = line

    for t in range(n_col * per):
        if t < TILES:
            rt, lt = t // 6, t % 6
            tile = gs[rt * 16 : rt * 16 + 16, lt * 128 : lt * 128 + 128].astype(BF16)
        else:
            tile = jnp.zeros((16, 128), BF16)
        sbuf[t // per, t % per * 16 : t % per * 16 + 16, :] = tile

    def scatter(peer, slot):
        return pltpu.make_async_remote_copy(
            src_ref=sbuf.at[peer], dst_ref=rbuf.at[slot], send_sem=ss1.at[peer],
            recv_sem=rs1.at[slot], device_id=(my_r, peer), device_id_type=MESH)

    def send1(k, _):
        scatter(lax.rem(my_c + k, n_col), my_c).start()
        return 0

    lax.fori_loop(1, n_col, send1, 0)
    rbuf[my_c] = sbuf[my_c]

    def to_lanes(value, stage, dst):
        stage[...] = value

        def one(w, _):
            lanes = pl.ds(pl.multiple_of(EDGE + w * SPAN, 128), SPAN)
            rows = pl.ds(pl.multiple_of(w * CELLS, CELLS), CELLS)
            first = stage[rows, 0:128]
            second = jnp.concatenate(
                [stage[rows, 128:WIDTH], jnp.zeros((CELLS, 256 - WIDTH), F32)], 1)
            dst[:, lanes] = join_tokens(first, second)
            return 0

        lax.fori_loop(0, WINDOWS, one, 0)

    d_normed = d_hidden * gain
    x = xs[...]
    center = x - jnp.mean(x, 1, keepdims=True)
    inv_std = lax.rsqrt(jnp.mean(center * center, 1, keepdims=True) + EPS)
    d_tokens = cs[...] + inv_std * (
        d_normed
        - jnp.mean(d_normed, 1, keepdims=True)
        - normed * jnp.mean(d_normed * normed, 1, keepdims=True))
    to_lanes(x + dot(att[...], wproj[...]) + bproj[...], xs, field)
    to_lanes(d_tokens, cs, cfield)
    for i, src in enumerate((field, cfield)):
        half = slice(i * WIN, i * WIN + WIN)
        orow[half, :] = pack_rows(src[:, :LANES]).astype(BF16)
        ocol[half, :] = src[:, LANES:].astype(BF16)
    for copy in lead:
        copy.wait_send()
    for copy in trail:
        copy.start()

    def recv1(k, _):
        peer = lax.rem(my_c + k, n_col)
        scatter(peer, peer).wait_recv()
        return 0

    lax.fori_loop(1, n_col, recv1, 0)
    acc = rbuf[0].astype(F32)
    for j in range(1, n_col):
        acc = acc + rbuf[j].astype(F32)
    acc = acc.astype(BF16)
    for i in range(per):
        s2[i] = acc[i * 16 : i * 16 + 16]

    gap = max(n_row // per, 1)
    slots = r2.shape[0]

    def owner(i):
        return lax.rem(i * gap + 2 * my_c, n_row)

    def up(i, device, slot):
        return pltpu.make_async_remote_copy(
            src_ref=s2.at[i], dst_ref=r2.at[i % slots, slot], send_sem=ss2.at[i],
            recv_sem=rs2.at[i % slots, slot], device_id=(device, my_c), device_id_type=MESH)

    def down(i, peer):
        return pltpu.make_async_remote_copy(
            src_ref=g2.at[i], dst_ref=g2.at[i], send_sem=ss3.at[peer],
            recv_sem=rs3.at[i], device_id=(peer, my_c), device_id_type=MESH)

    for i in range(per):
        @pl.when(owner(i) != my_r)
        def _():
            up(i, owner(i), my_r).start()

    for copy in trail:
        copy.wait_recv()
    for i, (src, dst) in enumerate(((field, res), (cfield, gin))):
        half = slice(i * WIN, i * WIN + WIN)
        low, high = merge_rows(rrow[half, :].astype(F32), src[:, :LANES])
        corner = jnp.where(
            upper((WIN, EDGE)), rdiag[half, :].astype(F32), rcol[half, :].astype(F32))
        dst[:, :EDGE] = corner.astype(BF16)
        dst[:, EDGE:HALF] = low[:, EDGE:].astype(BF16)
        dst[:, HALF:] = high.astype(BF16)

    for i in range(per):
        @pl.when(owner(i) == my_r)
        def _():
            slot = i % slots
            r2[slot, my_r] = s2[i]

            def recv2(k, _):
                peer = lax.rem(my_r + k, n_row)
                up(i, peer, peer).wait_recv()
                return 0

            lax.fori_loop(1, n_row, recv2, 0)
            total = r2[slot, 0].astype(F32)
            for j in range(1, n_row):
                total = total + r2[slot, j].astype(F32)
            g2[i] = total.astype(BF16)

            def send3(k, _):
                down(i, lax.rem(my_r + k, n_row)).start()
                return 0

            lax.fori_loop(1, n_row, send3, 0)

    for i in range(per):
        @pl.when(owner(i) != my_r)
        def _():
            down(i, my_r).wait_recv()

    def gather(peer, slot):
        return pltpu.make_async_remote_copy(
            src_ref=g2, dst_ref=fbuf.at[slot], send_sem=ss4.at[peer],
            recv_sem=rs4.at[slot], device_id=(my_r, peer), device_id_type=MESH)

    def send4(k, _):
        gather(lax.rem(my_c + k, n_col), my_c).start()
        return 0

    lax.fori_loop(1, n_col, send4, 0)
    fbuf[my_c] = g2[...]

    def recv4(k, _):
        peer = lax.rem(my_c + k, n_col)
        gather(peer, peer).wait_recv()
        return 0

    lax.fori_loop(1, n_col, recv4, 0)
    for t in range(TILES):
        rt, lt = t // 6, t % 6
        gs[rt * 16 : rt * 16 + 16, lt * 128 : lt * 128 + 128] = (
            fbuf[t // per, t % per].astype(F32) * grad_scale)
    g_qkv_w[...] = gs[0:WIDTH, : 3 * WIDTH]
    g_proj_w[...] = gs[0:WIDTH, 3 * WIDTH :]
    g_qkv_b[...] = gs[WIDTH : WIDTH + 1, : 3 * WIDTH]
    g_proj_b[...] = gs[WIDTH : WIDTH + 1, 3 * WIDTH :]
    g_gain[...] = gs[WIDTH + 1 : WIDTH + 2, :WIDTH]
    g_shift[...] = gs[WIDTH + 1 : WIDTH + 2, WIDTH : 2 * WIDTH]
    g_table[...] = gs[WIDTH + 2 : WIDTH + 2 + HEADS, :RELS]

    for copy in trail:
        copy.wait_send()

    def drain1(k, _):
        peer = lax.rem(my_c + k, n_col)
        scatter(peer, peer).wait_send()
        gather(peer, peer).wait_send()
        return 0

    lax.fori_loop(1, n_col, drain1, 0)
    for i in range(per):
        @pl.when(owner(i) != my_r)
        def _():
            up(i, owner(i), my_r).wait_send()

        @pl.when(owner(i) == my_r)
        def _():
            def drain3(k, _):
                down(i, lax.rem(my_r + k, n_row)).wait_send()
                return 0

            lax.fori_loop(1, n_row, drain3, 0)


def shards(image, cotangent, qkv_weight, qkv_bias, proj_weight, proj_bias, norm_gain, norm_bias,
           bias_table):
    n_row, n_col = lax.axis_size("row"), lax.axis_size("col")
    per = -(-TILES // n_col)
    slots = 1 if n_row >= per else per
    factor = float(n_row * n_col * TOKENS_HERE) ** (-0.5)
    tile = jax.ShapeDtypeStruct(image.shape, BF16)

    def line(width):
        return jax.ShapeDtypeStruct((1, width), F32)

    vmem = pl.BlockSpec(memory_space=pltpu.VMEM)
    dma = pltpu.SemaphoreType.DMA
    tokens = (TOKENS_HERE, WIDTH)
    halo = [pltpu.VMEM((16, HALF), BF16), pltpu.VMEM((16, EDGE), BF16)]
    arrived = [pltpu.VMEM((16, HALF), BF16)] + [pltpu.VMEM((16, EDGE), BF16)] * 2
    outs = pl.pallas_call(
        functools.partial(block_kernel, n_row, n_col, per, factor),
        out_shape=(
            tile, tile,
            jax.ShapeDtypeStruct((WIDTH, 3 * WIDTH), F32), line(3 * WIDTH),
            jax.ShapeDtypeStruct((WIDTH, WIDTH), F32), line(WIDTH),
            line(WIDTH), line(WIDTH), jax.ShapeDtypeStruct((HEADS, RELS), F32)),
        in_specs=[vmem] * 9,
        out_specs=(vmem,) * 9,
        scratch_shapes=halo + arrived + halo + arrived + [
            pltpu.VMEM((WIN, LANES + EDGE), F32), pltpu.VMEM((WIN, LANES + EDGE), F32),
            pltpu.VMEM(tokens, F32), pltpu.VMEM(tokens, F32), pltpu.VMEM(tokens, F32),
            pltpu.VMEM(tokens, BF16),
            pltpu.VMEM(tokens, BF16), pltpu.VMEM(tokens, BF16), pltpu.VMEM(tokens, BF16),
            pltpu.VMEM(tokens, BF16), pltpu.VMEM(tokens, BF16),
            pltpu.VMEM(tokens, F32), pltpu.VMEM(tokens, F32), pltpu.VMEM(tokens, F32),
            pltpu.VMEM((CELLS, HEADS * CELLS), F32),
            pltpu.VMEM((2, CELLS, HEADS * CELLS), F32),
            pltpu.VMEM((WIN, 256, 128), BF16),
            pltpu.VMEM((8, 256), F32),
            pltpu.VMEM((HEADS, WIN, 128), F32),
            pltpu.VMEM((WIDTH + 16, 4 * WIDTH), F32),
            pltpu.VMEM((n_col, per * 16, 128), BF16),
            pltpu.VMEM((n_col, per * 16, 128), BF16),
            pltpu.VMEM((per, 16, 128), BF16),
            pltpu.VMEM((slots, n_row, 16, 128), BF16),
            pltpu.VMEM((per, 16, 128), BF16),
            pltpu.VMEM((n_col, per, 16, 128), BF16),
            dma((6,)), dma((6,)), dma((n_col,)), dma((n_col,)), dma((per,)),
            dma((slots, n_row)), dma((n_row,)), dma((per,)), dma((n_col,)), dma((n_col,)),
        ],
        compiler_params=pltpu.CompilerParams(
            collective_id=1, has_side_effects=True, vmem_limit_bytes=48 * 1024 * 1024),
    )(image, cotangent, qkv_weight, qkv_bias[None], proj_weight, proj_bias[None], norm_gain[None],
      norm_bias[None], bias_table)
    return tuple(o[0] if o.shape[0] == 1 else o for o in outs)


def solution(mesh):
    in_specs = (P("row", "col"), P("row", "col"), P(), P(), P(), P(), P(), P(), P())
    out_specs = (P("row", "col"), P("row", "col"), P(), P(), P(), P(), P(), P(), P())
    return jax.shard_map(shards, mesh=mesh, in_specs=in_specs, out_specs=out_specs, check_vma=False)
```

time: 117 us -> 77.2 us (0.66)
  starting transfers between devices: 40.1 us -> 0 us
  Pallas kernels: 35.4 us -> 65.4 us
  matrix products: 19.7 us -> 0 us
  local copies, waits for them, and re-layouts: 14.8 us -> 10.2 us
  other arithmetic: 4.59 us -> 0.61 us
    ppermute x8 -> x0, starting transfers between devices: 40.1 us -> none  [passed_along(): return lax.ppermute(value, axis, pairs)]
    pallas_call x1, Pallas kernels: 35.4 us -> 65.4 us  [shards(): pl.pallas_call(functools.partial(block_kernel, n_row, n_col, per, factor)...]
    dot_general x13 -> x0, matrix products: 17.9 us -> none  [the longest x11 8.1 us: product(): return jnp.einsum(spec, left, right, preferred_element_type=jnp.float32)]
    slice x13 -> x0, local copies, waits for them, and re-layouts: 8.05 us -> none  [the longest x2 2.25 us: roll_lead(): stacked = jnp.concatenate([stacked[:, SHIFT:], arrived], 1)]
    unnamed x28 -> x24, local copies, waits for them, and re-layouts: 2.07 us -> 9.49 us
    reshape x4 -> x0, local copies, waits for them, and re-layouts: 2.18 us -> none  [the longest x1 1.45 us: backward(): d_value.reshape(shape_out)]
    sub x1 -> x0, matrix products: 1.82 us -> none  [forward(): expo = jnp.exp(scores - row_max)]
    squeeze x2 -> x0, other arithmetic: 1.54 us -> none  [the longest x1 0.77 us: shards(): grad_input = roll_trail(back_tile[None])[0]]
  transfers between devices with their start and end apart: 8 -> 0, of which waited for: 0 -> 0; matrix products, arithmetic and copies ran while one was open for 12% -> 0% of each run, Pallas kernels for 0% -> 0%
where the time goes in v2:
time: 77.2 us; the launch traced here: 76.9 us
  Pallas kernels  65.4 us (85%)
  local copies, waits for them, and re-layouts  10.2 us (13%)
    pallas_call x1, Pallas kernels, shards(): pl.pallas_call(functools.partial(block_kernel, n_row, n_col, per, factor)...  65.4 us
    unnamed x24, local copies, waits for them, and re-layouts  9.49 us

profile of v2, /device:TPU:1, one launch (start us, length us, event | category | flops | bytes accessed | tf_op | source)
XLA Modules:
  0.0 76.9 jit_solution(2830339756485753349)
XLA Ops:
  0.6 0.0 copy-start.4
  0.7 0.7 broadcast_in_dim.12.refs_3_
  1.3 0.0 copy-start.6
  1.3 0.0 copy-start.7
  1.4 0.0 copy-start.5
  1.4 0.0 copy-done.4
  1.4 0.7 copy-done.6
  2.0 0.0 copy-done.7
  2.0 0.0 copy-done.5
  2.1 0.0 copy-start
  2.1 0.9 %copy-done = bf16[192,576]{1,0:T(8,128)(2,1)S(1)} copy-done((bf16[192,576]{1,0:T(8,128)(2,1)S(1)}, bf16[192,576]{1,0:T(8,128)(2,1)}, u32[]{:S(2)}) %copy-start) | copy-done | bytes 221208
  3.0 0.9 %copy-done.1 = bf16[8,12288]{1,0:T(8,128)(2,1)S(1)} copy-done((bf16[8,12288]{1,0:T(8,128)(2,1)S(1)}, bf16[8,12288]{1,0:T(8,128)(2,1)}, u32[]{:S(2)}) %copy-start.1) | copy-done | bytes 196632
  3.9 0.9 %copy-done.2 = bf16[8,12288]{1,0:T(8,128)(2,1)S(1)} copy-done((bf16[8,12288]{1,0:T(8,128)(2,1)S(1)}, bf16[8,12288]{1,0:T(8,128)(2,1)}, u32[]{:S(2)}) %copy-start.2) | copy-done | bytes 196632
  4.9 0.9 %copy-done.3 = bf16[192,192]{1,0:T(8,128)(2,1)S(1)} copy-done((bf16[192,192]{1,0:T(8,128)(2,1)S(1)}, bf16[192,192]{1,0:T(8,128)(2,1)}, u32[]{:S(2)}) %copy-start.3) | copy-done | bytes 73752
  5.8 65.4 %shard_map.160 = (bf16[8,12288]{1,0:T(8,128)(2,1)S(1)}, bf16[8,12288]{1,0:T(8,128)(2,1)S(1)}, f32[192,576]{1,0:T(8,128)S(1)}, f32[1,576]{1,0:T(1,128)S(1)}, f32[...) custom-call(bf16[8,12288]{1,0:T(8,128)(2,1)S(1)} %copy-done.1, ...), custom_call_target="tpu_custom_call" | custom-call | tf_op jit(solution)/shard_map/pallas_call | solution.py:489
  71.2 0.6 reduce
  71.8 0.7 copy.26
  72.5 0.7 copy.27
  73.1 0.8 %copy.28 = f32[192,576]{1,0:T(8,128)} copy(f32[192,576]{1,0:T(8,128)S(1)} %get-tuple-element.38) | data formatting | bytes 884736
  73.9 0.7 copy.29
  74.6 0.6 copy.30
  75.2 0.6 copy.31
  75.7 0.6 copy.32
  76.3 0.6 copy.33
  (3 shorter events, 0.0 us)
Async XLA Ops:
  0.6 0.7 copy-start.4
  1.3 0.7 copy-start.6
  1.3 0.7 copy-start.7
  1.4 0.7 copy-start.5
  2.1 0.9 %copy-start = (bf16[192,576]{1,0:T(8,128)(2,1)S(1)}, bf16[192,576]{1,0:T(8,128)(2,1)}, u32[]{:S(2)}) copy-start(bf16[192,576]{1,0:T(8,128)(2,1)} %refs_2_.1) | copy-start | bytes 663556
  3.0 0.9 %copy-start.1 = (bf16[8,12288]{1,0:T(8,128)(2,1)S(1)}, bf16[8,12288]{1,0:T(8,128)(2,1)}, u32[]{:S(2)}) copy-start(bf16[8,12288]{1,0:T(8,128)(2,1)} %refs_0_.1) | copy-start | bytes 589828
  3.9 0.9 %copy-start.2 = (bf16[8,12288]{1,0:T(8,128)(2,1)S(1)}, bf16[8,12288]{1,0:T(8,128)(2,1)}, u32[]{:S(2)}) copy-start(bf16[8,12288]{1,0:T(8,128)(2,1)} %refs_1_.1) | copy-start | bytes 589828
  4.9 0.9 %copy-start.3 = (bf16[192,192]{1,0:T(8,128)(2,1)S(1)}, bf16[192,192]{1,0:T(8,128)(2,1)}, u32[]{:S(2)}) copy-start(bf16[192,192]{1,0:T(8,128)(2,1)} %refs_4_.1) | copy-start | bytes 221188

commit v3 on v2

v3 whole, which is shorter than its diff:
```python
import functools

import jax
import jax.numpy as jnp
from jax import lax
from jax.experimental import pallas as pl
from jax.experimental.pallas import tpu as pltpu
from jax.sharding import PartitionSpec as P

WIDTH = 192
HEADS = 6
HEAD_DIM = 32
WIN = 8
CELLS = WIN * WIN
SHIFT = 4
RELS = 225
EPS = 1e-05
NEG = -1e30
TILE_COLS = 64
LANES = TILE_COLS * WIDTH
EDGE = SHIFT * WIDTH
WINDOWS = TILE_COLS // WIN
SPAN = WIN * WIDTH
TOKENS_HERE = WINDOWS * CELLS
CHUNKS = 4
PER_CHUNK = WINDOWS // CHUNKS
CHUNK_TOKENS = PER_CHUNK * CELLS
CHUNK = PER_CHUNK * SPAN
HALF = CHUNK // 2
SCALE = HEAD_DIM**-0.5
GROUPS = ((0, 4), (4, 2))
STRIPES = 13
WIDE = 4 * WIDTH
MID = WIDE // 2

MESH = pl.DeviceIdType.MESH
F32 = jnp.float32
BF16 = jnp.bfloat16


def dot(a, b, ca=1, cb=0):
    return lax.dot_general(a, b, (((ca,), (cb,)), ((), ())), preferred_element_type=F32)


def iota(shape, dim):
    return lax.broadcasted_iota(jnp.int32, shape, dim)


def upper(shape):
    return iota(shape, 0) < SHIFT


def pack_rows(field):
    back = pltpu.roll(field[:, HALF:], SHIFT, 0)
    return jnp.where(upper((WIN, HALF)), field[:, :HALF], back)


def merge_rows(packed, field):
    low = jnp.where(upper((WIN, HALF)), packed, field[:, :HALF])
    high = jnp.where(upper((WIN, HALF)), pltpu.roll(packed, SHIFT, 0), field[:, HALF:])
    return jnp.concatenate([low, high], 1)


def split_tokens(strip):
    left = iota((WIN, 128), 1) < 64
    first, second = [], []
    for j in range(WIN // 2):
        v = [strip[:, (3 * j + i) * 128 : (3 * j + i + 1) * 128] for i in range(3)]
        r1, r2 = pltpu.roll(v[1], 64, 1), pltpu.roll(v[2], 64, 1)
        first += [v[0], jnp.where(left, r1, r2)]
        second += [v[1], r2]
    return jnp.concatenate(first, 0), jnp.concatenate(second, 0)


def join_tokens(first, second):
    left = iota((WIN, 128), 1) < 64
    out = []
    for j in range(WIN // 2):
        e = slice(16 * j, 16 * j + 8)
        o = slice(16 * j + 8, 16 * j + 16)
        swapped = pltpu.roll(first[o], 64, 1)
        out.append(first[e])
        out.append(jnp.where(left, second[e], swapped))
        out.append(jnp.where(left, swapped, pltpu.roll(second[o], 64, 1)))
    return jnp.concatenate(out, 1)


def build_bias(table_ref, onehot, padded, diag, bias, last_row, last_col):
    padded[...] = jnp.zeros((8, 256), F32)
    padded[0:HEADS, 0:RELS] = table_ref[...]
    table = padded[...]
    hi = table.astype(BF16)
    rest = table - hi.astype(F32)
    mid = rest.astype(BF16)
    low = (rest - mid.astype(F32)).astype(BF16)
    lane = iota((1, 128), 1)
    a_q = (lane + SHIFT) % WIN
    for a in range(WIN):
        target = (a_q - (a + SHIFT) % WIN + WIN - 1) * (2 * WIN - 1) + lane // WIN
        target = jnp.where(lane < 120, target, -1)
        hot = jnp.where(iota((256, 128), 0) == target, 1.0, 0.0).astype(BF16)
        onehot[a] = hot
        rows = dot(hi, hot) + dot(mid, hot) + dot(low, hot)
        for h in range(HEADS):
            diag[h, a : a + 1, :] = rows[h : h + 1, :]
    sub = iota((WIN, 128), 0)
    lanes = iota((WIN, 128), 1)
    row_cut = jnp.where((sub < SHIFT) != (lanes % WIN < SHIFT), NEG, 0.0) * last_row
    right = lanes % 64 // WIN >= SHIFT
    for b in range(WIN):
        col_cut = jnp.where(right != (b >= SHIFT), NEG, 0.0) * last_col
        for pair in range(HEADS // 2):
            shift = (WIN - 1 - b) * WIN
            even = pltpu.roll(diag[2 * pair], (128 - shift) % 128, 1)
            odd = pltpu.roll(diag[2 * pair + 1], (192 - shift) % 128, 1)
            block = jnp.where(lanes < 64, even, odd) + row_cut
            where = (slice(b * WIN, b * WIN + WIN), slice(pair * 128, pair * 128 + 128))
            bias[(0,) + where] = block
            bias[(1,) + where] = block + col_cut


def table_grad(total, onehot, diag):
    lanes = iota((WIN, 128), 1)
    for h in range(HEADS):
        mine = (lanes < 64) == (h % 2 == 0)
        acc = jnp.zeros((WIN, 128), F32)
        for b in range(WIN):
            block = total[b * WIN : b * WIN + WIN, h // 2 * 128 : h // 2 * 128 + 128]
            block = jnp.where(mine, block, 0.0)
            acc = acc + pltpu.roll(block, ((WIN - 1 - b) * WIN + h % 2 * 64) % 128, 1)
        diag[h] = acc
    flat = jnp.concatenate([diag[h] for h in range(HEADS)], 0)
    hi = flat.astype(BF16)
    low = (flat - hi.astype(F32)).astype(BF16)
    sub = iota((HEADS * WIN, 256), 0) % WIN
    acc = jnp.zeros((HEADS * WIN, 256), F32)
    for a in range(WIN):
        part = dot(hi, onehot[a], 1, 1) + dot(low, onehot[a], 1, 1)
        acc = acc + jnp.where(sub == a, part, 0.0)
    return [
        jnp.sum(acc[h * WIN : h * WIN + WIN], 0, keepdims=True) for h in range(HEADS)
    ]


def masked_heads(x, group):
    start, count = group
    lane = iota((CELLS, count * HEAD_DIM), 1) // HEAD_DIM
    wide = x[:, start * HEAD_DIM : (start + count) * HEAD_DIM]
    zero = jnp.zeros_like(wide)
    return jnp.concatenate([jnp.where(lane == h, wide, zero) for h in range(count)], 0)


def own_heads(x, count):
    lane = iota((CELLS, count * HEAD_DIM), 1) // HEAD_DIM
    out = x[(count - 1) * CELLS : count * CELLS]
    for h in range(count - 1):
        out = jnp.where(lane == h, x[h * CELLS : (h + 1) * CELLS], out)
    return out


def fold(x):
    return jnp.sum(x.reshape(-1, WIN, x.shape[1]), 0)


def window_step(q, k, v, da, bias, gsum):
    att, dq, dk, dv = [], [], [], []
    for start, count in GROUPS:
        ch = slice(start * HEAD_DIM, (start + count) * HEAD_DIM)
        lanes = slice(start * CELLS, (start + count) * CELLS)
        qm = masked_heads(q, (start, count))
        dam = masked_heads(da, (start, count))
        s = dot(k[:, ch], qm, 1, 1) * SCALE + bias[:, lanes]
        e = jnp.exp(s - jnp.max(s, 0, keepdims=True))
        p = e * (1.0 / jnp.sum(e, 0, keepdims=True))
        dp = dot(v[:, ch], dam, 1, 1)
        ds = p * (dp - jnp.sum(p * dp, 0, keepdims=True))
        gsum[:, lanes] += ds
        pb, dsb = p.astype(BF16), ds.astype(BF16)
        dv.append(dot(pb, dam))
        dk.append(dot(dsb, qm) * SCALE)
        att.append(own_heads(dot(pb, v[:, ch], 0, 0), count).astype(BF16))
        dq.append(own_heads(dot(dsb, k[:, ch], 0, 0), count) * SCALE)
    return [jnp.concatenate(parts, 1) for parts in (att, dq, dk, dv)]


def block_kernel(n_row, n_col, spp, grad_scale, *refs):
    (img_h, cot_h, wqkv_h, bqkv_h, wproj_h, bproj_h, gain_h, shift_h, table_h,
     res, gin, total_out,
     img, cot, wqkv, bqkv, wproj, bproj, gain_ref, shift_ref, table_ref,
     irow, icol, hrow, hcol, hdiag, orow, ocol, rrow, rcol, rdiag,
     field, cfield, corner, weights, xd, xhid, xatt, sums, gsum,
     bias, onehot, padded, diag, gs, c_out, c_in, plane_buf, p_in, z_out, z_in, half_buf, last_in,
     ls, hs, hr, cs_sem, cr_sem, ps, pr, zs, zr, as_sem, ar_sem) = refs
    my_r, my_c = lax.axis_index("row"), lax.axis_index("col")
    above, below = lax.rem(my_r + n_row - 1, n_row), lax.rem(my_r + 1, n_row)
    left, right = lax.rem(my_c + n_col - 1, n_col), lax.rem(my_c + 1, n_col)
    n_plane, n_z = n_col, n_row // 2
    core = lax.rem(my_c, 2)
    my_p = my_c // 2 * 2 + lax.rem(my_r, 2)
    my_z = my_r // 2
    owners = -(-STRIPES // spp)
    rows_each = spp * 16

    def plane_peer(p):
        return (my_z * 2 + lax.rem(p, 2), p // 2 * 2 + core)

    def z_peer(z):
        return (z * 2 + lax.rem(my_r, 2), my_c)

    local = [
        pltpu.make_async_copy(src, dst, ls.at[i])
        for i, (src, dst) in enumerate((
            (img_h, img), (cot_h, cot), (wqkv_h, wqkv), (bqkv_h, bqkv), (wproj_h, wproj),
            (bproj_h, bproj), (gain_h, gain_ref), (shift_h, shift_ref), (table_h, table_ref)))
    ]
    for copy in local:
        copy.start()
    barrier = pltpu.get_barrier_semaphore()

    def greet(device):
        pl.semaphore_signal(barrier, inc=1, device_id=device, device_id_type=MESH)

    def greet_z(k, _):
        greet(z_peer(lax.rem(my_z + k, n_z)))
        return 0

    def greet_plane(k, _):
        greet(plane_peer(lax.rem(my_p + k, n_plane)))
        return 0

    lax.fori_loop(1, n_z, greet_z, 0)
    lax.fori_loop(1, n_plane, greet_plane, 0)
    for device in ((above, my_c), (below, my_c), (my_r, left), (my_r, right), (above, left),
                   (below, right)):
        greet(device)

    def remote(src, dst, send, recv, device):
        return pltpu.make_async_remote_copy(
            src_ref=src, dst_ref=dst, send_sem=send, recv_sem=recv, device_id=device,
            device_id_type=MESH)

    def halo(src, dst, i, device):
        return remote(src, dst, hs.at[i], hr.at[i], device)

    def lead_row(g):
        return halo(irow.at[g], hrow.at[g], g, (above, my_c))

    def trail_row(g):
        return halo(orow.at[g], rrow.at[g], CHUNKS + g, (below, my_c))

    n = 2 * CHUNKS
    lead = (halo(icol, hcol, n, (my_r, left)), halo(icol, hdiag, n + 1, (above, left)))
    trail = (halo(ocol, rcol, n + 2, (my_r, right)), halo(ocol, rdiag, n + 3, (below, right)))

    local[0].wait()
    local[1].wait()
    for i, (src, dst) in enumerate(((img, field), (cot, cfield))):
        half = slice(i * WIN, i * WIN + WIN)
        tile = src[...].astype(F32)
        icol[half, :] = tile[:, :EDGE].astype(BF16)
        dst[:, :LANES] = tile
        dst[:, LANES:] = tile[:, :EDGE]
        for g in range(CHUNKS):
            lanes = slice(EDGE + g * CHUNK, EDGE + (g + 1) * CHUNK)
            irow[g, half, :] = pack_rows(dst[:, lanes]).astype(BF16)
    pl.semaphore_wait(barrier, n_z - 1 + n_plane - 1 + 6)
    for g in range(CHUNKS):
        lead_row(g).start()
    for copy in lead:
        copy.start()

    for copy in local[2:]:
        copy.wait()
    last_row = (my_r == n_row - 1).astype(F32)
    last_col = (my_c == n_col - 1).astype(F32)
    build_bias(table_ref, onehot, padded, diag, bias, last_row, last_col)
    gsum[...] = jnp.zeros_like(gsum)
    sums[...] = jnp.zeros_like(sums)
    gs[WIDTH:, :] = jnp.zeros((owners * rows_each - WIDTH, WIDE), F32)
    for i in range(3):
        weights[i] = wqkv[:, i * WIDTH : (i + 1) * WIDTH]
    qkv_bias = bqkv[...].reshape(1, 3 * WIDTH)
    biases = [qkv_bias[:, i * WIDTH : (i + 1) * WIDTH] for i in range(3)]
    proj_bias = bproj[...].reshape(1, WIDTH)
    gain = gain_ref[...].reshape(1, WIDTH)
    shift = shift_ref[...].reshape(1, WIDTH)

    for copy in lead:
        copy.wait_recv()
    for i in range(2):
        half = slice(i * WIN, i * WIN + WIN)
        corner[i] = jnp.where(
            upper((WIN, EDGE)), hdiag[half, :].astype(F32), hcol[half, :].astype(F32))

    def chunk_step(g, _):
        final = g == CHUNKS - 1
        lanes = pl.ds(pl.multiple_of(EDGE + g * CHUNK, 128), CHUNK)
        rows = pl.ds(pl.multiple_of(g * CHUNK_TOKENS, CHUNK_TOKENS), CHUNK_TOKENS)
        lead_row(g).wait_recv()
        tokens = []
        for i, src in enumerate((field, cfield)):
            half = slice(i * WIN, i * WIN + WIN)
            whole = merge_rows(hrow[g, half, :].astype(F32), src[:, lanes])
            end = jnp.where(final, corner[i], whole[:, CHUNK - EDGE :])
            whole = jnp.concatenate([whole[:, : CHUNK - EDGE], end], 1)
            parts = [split_tokens(whole[:, j * SPAN : (j + 1) * SPAN]) for j in range(PER_CHUNK)]
            first = jnp.concatenate([part[0] for part in parts], 0)
            second = jnp.concatenate([part[1] for part in parts], 0)
            tokens.append(jnp.concatenate([first, second[:, : WIDTH - 128]], 1))
        x, cot_f = tokens
        center = x - jnp.mean(x, 1, keepdims=True)
        inv_std = lax.rsqrt(jnp.mean(center * center, 1, keepdims=True) + EPS)
        normed = center * inv_std
        hidden = (normed * gain + shift).astype(BF16)
        xhid[rows, :] = hidden
        q, k, v = [(dot(hidden, weights[i]) + biases[i]).astype(BF16) for i in range(3)]
        cot_b = cot_f.astype(BF16)
        da = dot(cot_b, wproj[...], 1, 1).astype(BF16)
        found = []
        for j in range(PER_CHUNK):
            r = slice(j * CELLS, (j + 1) * CELLS)
            if j == PER_CHUNK - 1:
                add = bias.at[final.astype(jnp.int32)]
            else:
                add = bias.at[0]
            found.append(window_step(q[r], k[r], v[r], da[r], add, gsum))
        att, dq, dk, dv = [jnp.concatenate([part[i] for part in found], 0) for i in range(4)]
        xatt[rows, :] = att
        out = x + dot(att, wproj[...]) + proj_bias
        d_hidden = jnp.zeros((CHUNK_TOKENS, WIDTH), F32)
        for i, part in enumerate((dq, dk, dv)):
            part_b = part.astype(BF16)
            xd[i, rows, :] = part_b
            sums[i] += fold(part)
            d_hidden = d_hidden + dot(part_b, weights[i], 1, 1)
        xd[3, rows, :] = cot_b
        sums[3] += fold(cot_f)
        sums[4] += fold(d_hidden * normed)
        sums[5] += fold(d_hidden)
        d_normed = d_hidden * gain
        d_tokens = cot_f + inv_std * (
            d_normed
            - jnp.mean(d_normed, 1, keepdims=True)
            - normed * jnp.mean(d_normed * normed, 1, keepdims=True))
        for i, (value, dst) in enumerate(((out, field), (d_tokens, cfield))):
            half = slice(i * WIN, i * WIN + WIN)
            first = value[:, :128]
            second = jnp.concatenate(
                [value[:, 128:], jnp.zeros((CHUNK_TOKENS, 256 - WIDTH), F32)], 1)
            strips = []
            for j in range(PER_CHUNK):
                r = slice(j * CELLS, (j + 1) * CELLS)
                strips.append(join_tokens(first[r], second[r]))
            whole = jnp.concatenate(strips, 1)
            dst[:, lanes] = whole
            orow[g, half, :] = pack_rows(whole).astype(BF16)
            ocol[half, :] = whole[:, CHUNK - EDGE :].astype(BF16)
        trail_row(g).start()
        return 0

    lax.fori_loop(0, CHUNKS, chunk_step, 0)
    for copy in trail:
        copy.start()

    hidden_t = xhid[...].T
    for i in range(3):
        gs[0:WIDTH, i * WIDTH : (i + 1) * WIDTH] = dot(hidden_t, xd[i])
    gs[0:WIDTH, 3 * WIDTH :] = dot(xatt[...], xd[3], 0, 0)
    for i in range(4):
        gs[WIDTH : WIDTH + 1, i * WIDTH : (i + 1) * WIDTH] = jnp.sum(sums[i], 0, keepdims=True)
    for i in range(2):
        gs[WIDTH + 1 : WIDTH + 2, i * WIDTH : (i + 1) * WIDTH] = jnp.sum(
            sums[4 + i], 0, keepdims=True)
    for h, line in enumerate(table_grad(gsum[...], onehot, diag)):
        gs[WIDTH + 2 + h : WIDTH + 3 + h, 0:256] = line

    mine = pl.ds(pl.multiple_of(core * MID, 128), MID)
    other = pl.ds(pl.multiple_of((1 - core) * MID, 128), MID)
    partner = (my_r, my_c + 1 - 2 * core)
    c_out[...] = gs[:, other].astype(BF16)
    swap = remote(c_out, c_in, cs_sem.at[0], cr_sem.at[0], partner)
    swap.start()
    swap.wait_recv()
    plane_buf[...] = (gs[:, mine] + c_in[...].astype(F32)).astype(BF16).reshape(
        owners, rows_each, MID)

    def scatter(p, slot):
        return remote(plane_buf.at[p], p_in.at[slot], ps.at[p], pr.at[slot], plane_peer(p))

    def from_plane(p):
        return remote(plane_buf.at[0], p_in.at[p], ps.at[0], pr.at[p], plane_peer(p))

    def send_scatter(k, _):
        p = lax.rem(my_p + k, n_plane)

        @pl.when(p < owners)
        def _():
            scatter(p, my_p).start()

        return 0

    lax.fori_loop(1, n_plane, send_scatter, 0)

    for g in range(CHUNKS):
        trail_row(g).wait_recv()
    for copy in trail:
        copy.wait_recv()
    for i, (src, dst) in enumerate(((field, res), (cfield, gin))):
        half = slice(i * WIN, i * WIN + WIN)
        ends = jnp.where(
            upper((WIN, EDGE)), rdiag[half, :].astype(F32), rcol[half, :].astype(F32))
        dst[:, :EDGE] = ends.astype(BF16)
        for g in range(CHUNKS):
            start = EDGE + g * CHUNK
            size = min(CHUNK, LANES - start)
            whole = merge_rows(rrow[g, half, :].astype(F32), src[:, start : start + CHUNK])
            dst[:, start : start + size] = whole[:, :size].astype(BF16)

    def along_z(z, slot):
        return remote(z_out, z_in.at[slot], zs.at[z], zr.at[slot], z_peer(z))

    def spread(p, owner):
        return remote(half_buf.at[owner], half_buf.at[owner], as_sem.at[p], ar_sem.at[owner],
                      plane_peer(p))

    def loop_plane(step):
        def one(k, _):
            step(lax.rem(my_p + k, n_plane))
            return 0

        lax.fori_loop(1, n_plane, one, 0)

    def loop_z(step):
        def one(k, _):
            step(lax.rem(my_z + k, n_z))
            return 0

        lax.fori_loop(1, n_z, one, 0)

    @pl.when(my_p < owners)
    def _():
        p_in[my_p] = plane_buf[my_p]
        loop_plane(lambda p: from_plane(p).wait_recv())
        acc = p_in[0].astype(F32)
        for j in range(1, n_plane):
            acc = acc + p_in[j].astype(F32)
        z_out[...] = acc.astype(BF16)
        loop_z(lambda z: along_z(z, my_z).start())
        z_in[my_z] = z_out[...]
        loop_z(lambda z: along_z(z, z).wait_recv())
        acc = z_in[0].astype(F32)
        for j in range(1, n_z):
            acc = acc + z_in[j].astype(F32)
        half_buf[my_p] = acc.astype(BF16)
        loop_plane(lambda p: spread(p, my_p).start())

    def arrive(p):
        @pl.when(p < owners)
        def _():
            spread(p, p).wait_recv()

    loop_plane(arrive)
    back = remote(half_buf, last_in, cs_sem.at[1], cr_sem.at[1], partner)
    back.start()
    flat = (owners * rows_each, MID)
    total_out[:, mine] = half_buf[...].astype(F32).reshape(flat) * grad_scale
    back.wait_recv()
    total_out[:, other] = last_in[...].astype(F32).reshape(flat) * grad_scale

    for g in range(CHUNKS):
        lead_row(g).wait_send()
        trail_row(g).wait_send()
    for copy in lead + trail + (swap, back):
        copy.wait_send()

    def sent(p):
        @pl.when(p < owners)
        def _():
            scatter(p, my_p).wait_send()

    loop_plane(sent)

    @pl.when(my_p < owners)
    def _():
        loop_z(lambda z: along_z(z, my_z).wait_send())
        loop_plane(lambda p: spread(p, my_p).wait_send())


def finish_kernel(res, gin, total, *refs):
    outs, (b0, b1, w0, w1, v0, v1, v2, t0, sems) = refs[:9], refs[9:]
    w0[...] = total[0:WIDTH, : 3 * WIDTH]
    w1[...] = total[0:WIDTH, 3 * WIDTH :]
    b0[...] = total[WIDTH : WIDTH + 1, : 3 * WIDTH].reshape(3 * WIDTH)
    v0[...] = total[WIDTH : WIDTH + 1, 3 * WIDTH :].reshape(WIDTH)
    v1[...] = total[WIDTH + 1 : WIDTH + 2, :WIDTH].reshape(WIDTH)
    v2[...] = total[WIDTH + 1 : WIDTH + 2, WIDTH : 2 * WIDTH].reshape(WIDTH)
    t0[...] = total[WIDTH + 2 : WIDTH + 2 + HEADS, :RELS]
    copies = [
        pltpu.make_async_copy(src, dst, sems.at[i])
        for i, (src, dst) in enumerate(zip((res, gin, w0, b0, w1, v0, v1, v2, t0), outs))
    ]
    for copy in copies:
        copy.start()
    for copy in copies:
        copy.wait()


def shards(image, cotangent, qkv_weight, qkv_bias, proj_weight, proj_bias, norm_gain, norm_bias,
           bias_table):
    n_row, n_col = lax.axis_size("row"), lax.axis_size("col")
    spp = -(-STRIPES // n_col)
    owners = -(-STRIPES // spp)
    rows_each = spp * 16
    factor = float(n_row * n_col * TOKENS_HERE) ** (-0.5)
    args = (image, cotangent, qkv_weight, qkv_bias, proj_weight, proj_bias, norm_gain, norm_bias,
            bias_table)
    tile = jax.ShapeDtypeStruct(image.shape, BF16)
    vmem = pl.BlockSpec(memory_space=pltpu.VMEM)
    hbm = pl.BlockSpec(memory_space=pltpu.HBM)
    dma = pltpu.SemaphoreType.DMA
    row_halo = pltpu.VMEM((CHUNKS, 16, HALF), BF16)
    col_halo = pltpu.VMEM((16, EDGE), BF16)
    half = (owners * rows_each, MID)
    halves = (owners, rows_each, MID)
    stripe = (rows_each, MID)
    parts = pl.pallas_call(
        functools.partial(block_kernel, n_row, n_col, spp, factor),
        out_shape=(tile, tile, jax.ShapeDtypeStruct((owners * rows_each, WIDE), F32)),
        in_specs=[hbm] * 9,
        out_specs=(vmem,) * 3,
        scratch_shapes=[pltpu.VMEM(a.shape, a.dtype) for a in args]
        + [row_halo, col_halo, row_halo, col_halo, col_halo] * 2
        + [
            pltpu.VMEM((WIN, LANES + EDGE), F32), pltpu.VMEM((WIN, LANES + EDGE), F32),
            pltpu.VMEM((2, WIN, EDGE), F32),
            pltpu.VMEM((3, WIDTH, WIDTH), BF16),
            pltpu.VMEM((4, TOKENS_HERE, WIDTH), BF16),
            pltpu.VMEM((TOKENS_HERE, WIDTH), BF16),
            pltpu.VMEM((TOKENS_HERE, WIDTH), BF16),
            pltpu.VMEM((6, WIN, WIDTH), F32),
            pltpu.VMEM((CELLS, HEADS * CELLS), F32),
            pltpu.VMEM((2, CELLS, HEADS * CELLS), F32),
            pltpu.VMEM((WIN, 256, 128), BF16),
            pltpu.VMEM((8, 256), F32),
            pltpu.VMEM((HEADS, WIN, 128), F32),
            pltpu.VMEM((owners * rows_each, WIDE), F32),
            pltpu.VMEM(half, BF16), pltpu.VMEM(half, BF16),
            pltpu.VMEM(halves, BF16), pltpu.VMEM((n_col,) + stripe, BF16),
            pltpu.VMEM(stripe, BF16), pltpu.VMEM((n_row // 2,) + stripe, BF16),
            pltpu.VMEM(halves, BF16), pltpu.VMEM(halves, BF16),
            dma((9,)), dma((2 * CHUNKS + 4,)), dma((2 * CHUNKS + 4,)), dma((2,)), dma((2,)),
            dma((n_col,)), dma((n_col,)), dma((n_row // 2,)), dma((n_row // 2,)),
            dma((n_col,)), dma((n_col,)),
        ],
        compiler_params=pltpu.CompilerParams(
            collective_id=1, has_side_effects=True, vmem_limit_bytes=60 * 1024 * 1024),
    )(*args)
    shapes = (image, cotangent, (WIDTH, 3 * WIDTH), (3 * WIDTH,), (WIDTH, WIDTH), (WIDTH,),
              (WIDTH,), (WIDTH,), (HEADS, RELS))
    outs = (tile, tile) + tuple(jax.ShapeDtypeStruct(s, F32) for s in shapes[2:])
    stage = [shapes[3], (1,), shapes[2], shapes[4], shapes[5], shapes[6], shapes[7], shapes[8]]
    return pl.pallas_call(
        finish_kernel,
        out_shape=outs,
        in_specs=[vmem] * 3,
        out_specs=(hbm,) * 9,
        scratch_shapes=[pltpu.VMEM(s, F32) for s in stage] + [dma((9,))],
        compiler_params=pltpu.CompilerParams(vmem_limit_bytes=60 * 1024 * 1024),
    )(*parts)


def solution(mesh):
    in_specs = (P("row", "col"), P("row", "col"), P(), P(), P(), P(), P(), P(), P())
    out_specs = (P("row", "col"), P("row", "col"), P(), P(), P(), P(), P(), P(), P())
    return jax.shard_map(shards, mesh=mesh, in_specs=in_specs, out_specs=out_specs, check_vma=False)
```

time: 77.2 us -> 65 us (0.84)
  local copies, waits for them, and re-layouts: 10.2 us -> 0 us
  Pallas kernels: 65.4 us -> 64.2 us
    unnamed x24 -> x0, local copies, waits for them, and re-layouts: 9.49 us -> none
    pallas_call x1 -> x2, Pallas kernels: 65.4 us -> 64.2 us  [the longest x1 61.9 us: shards(): pl.pallas_call(functools.partial(block_kernel, n_row, n_col, spp, factor)...]
where the time goes in v3:
time: 65 us; the launch traced here: 64.9 us
  Pallas kernels  64.2 us (99%)
  between operations  0.65 us (1%)
    pallas_call x1, Pallas kernels, shards(): pl.pallas_call(functools.partial(block_kernel, n_row, n_col, spp, factor)...  61.9 us
    pallas_call x1, Pallas kernels, shards(): pl.pallas_call(finish_kernel, out_shape=outs, in_specs=[vmem] * 3, out_sp...  2.34 us

profile of v3, /device:TPU:1, one launch (start us, length us, event | category | flops | bytes accessed | tf_op | source)
XLA Modules:
  0.0 64.9 jit_solution(12475814906509315263)
XLA Ops:
  0.6 61.9 %shard_map.160 = (bf16[8,12288]{1,0:T(8,128)(2,1)}, bf16[8,12288]{1,0:T(8,128)(2,1)}, f32[208,768]{1,0:T(8,128)}) custom-call(bf16[8,12288]{1,0:T(8,128)(2,1)} %refs_0_.1, bf16[8,12288]{1,0:T(8,128)(2,1)} %refs_1_.1, bf16[192,576]{1,0:T(8,128)(2,1)} %refs_2_.1, f32[576]{0:T(1024)} %refs_3_.1, bf16[192,192]{1,0:T(8,128)(2,1)} %refs_4_.1, f32[192]{0:T(256)} %refs_5_.1, ...), custom_call_target="tpu_custom_call" | custom-call | tf_op jit(solution)/shard_map/pallas_call | solution.py:526
  62.5 2.3 %shard_map.161 = (bf16[8,12288]{1,0:T(8,128)(2,1)}, bf16[8,12288]{1,0:T(8,128)(2,1)}, f32[192,576]{1,0:T(8,128)}, f32[576]{0:T(1024)}, f32[192,192]{1,0:T(8,128)...) custom-call(bf16[8,12288]{1,0:T(8,128)(2,1)} %get-tuple-element.12.res, ...), custom_call_target="tpu_custom_call" | custom-call | tf_op jit(solution)/shard_map/pallas_call | solution.py:562

commit v4 on v3

--- a/solution.py
+++ b/solution.py
@@ -190,7 +190,8 @@
      irow, icol, hrow, hcol, hdiag, orow, ocol, rrow, rcol, rdiag,
      field, cfield, corner, weights, xd, xhid, xatt, sums, gsum,
      bias, onehot, padded, diag, gs, c_out, c_in, plane_buf, p_in, z_out, z_in, half_buf, last_in,
-     ls, hs, hr, cs_sem, cr_sem, ps, pr, zs, zr, as_sem, ar_sem) = refs
+     ls, hs, hr, cs_sem, cr_sem, ps, pr, zs, zr, as_sem, ar_sem,
+     row_known, col_known, pair_known) = refs
     my_r, my_c = lax.axis_index("row"), lax.axis_index("col")
     above, below = lax.rem(my_r + n_row - 1, n_row), lax.rem(my_r + 1, n_row)
     left, right = lax.rem(my_c + n_col - 1, n_col), lax.rem(my_c + 1, n_col)
@@ -220,19 +221,48 @@
     def greet(device):
         pl.semaphore_signal(barrier, inc=1, device_id=device, device_id_type=MESH)
 
-    def greet_z(k, _):
-        greet(z_peer(lax.rem(my_z + k, n_z)))
-        return 0
-
-    def greet_plane(k, _):
-        greet(plane_peer(lax.rem(my_p + k, n_plane)))
-        return 0
-
-    lax.fori_loop(1, n_z, greet_z, 0)
-    lax.fori_loop(1, n_plane, greet_plane, 0)
     for device in ((above, my_c), (below, my_c), (my_r, left), (my_r, right), (above, left),
                    (below, right)):
         greet(device)
+
+    rounds = [(g, 2**g) for g in range(CHUNKS)]
+    row_rounds = [(g, d) for g, d in rounds if 4 * d <= n_row]
+    col_rounds = [(g, d) for g, d in rounds if 4 * d <= n_col]
+
+    def tell(sem, device):
+        pl.semaphore_signal(sem, inc=1, device_id=device, device_id_type=MESH)
+
+    def start_round(g):
+        for k, d in row_rounds:
+            @pl.when(g == k)
+            def _():
+                tell(row_known.at[k], (lax.rem(my_r + d, n_row), my_c))
+                tell(row_known.at[k], (lax.rem(my_r + n_row - d, n_row), my_c))
+
+        for k, d in col_rounds:
+            @pl.when(g == k)
+            def _():
+                tell(col_known.at[k], (my_r, lax.rem(my_c + d, n_col)))
+                tell(col_known.at[k], (my_r, lax.rem(my_c + n_col - d, n_col)))
+
+        @pl.when(g == CHUNKS - 1)
+        def _():
+            tell(pair_known, (my_r + 1 - 2 * lax.rem(my_r, 2), my_c))
+
+    def end_round(g):
+        for k, _ in row_rounds:
+            @pl.when(g == k)
+            def _():
+                pl.semaphore_wait(row_known.at[k], 2)
+
+        for k, _ in col_rounds:
+            @pl.when(g == k)
+            def _():
+                pl.semaphore_wait(col_known.at[k], 2)
+
+        @pl.when(g == CHUNKS - 1)
+        def _():
+            pl.semaphore_wait(pair_known, 1)
 
     def remote(src, dst, send, recv, device):
         return pltpu.make_async_remote_copy(
@@ -263,7 +293,7 @@
         for g in range(CHUNKS):
             lanes = slice(EDGE + g * CHUNK, EDGE + (g + 1) * CHUNK)
             irow[g, half, :] = pack_rows(dst[:, lanes]).astype(BF16)
-    pl.semaphore_wait(barrier, n_z - 1 + n_plane - 1 + 6)
+    pl.semaphore_wait(barrier, 6)
     for g in range(CHUNKS):
         lead_row(g).start()
     for copy in lead:
@@ -296,6 +326,7 @@
         final = g == CHUNKS - 1
         lanes = pl.ds(pl.multiple_of(EDGE + g * CHUNK, 128), CHUNK)
         rows = pl.ds(pl.multiple_of(g * CHUNK_TOKENS, CHUNK_TOKENS), CHUNK_TOKENS)
+        start_round(g)
         lead_row(g).wait_recv()
         tokens = []
         for i, src in enumerate((field, cfield)):
@@ -356,6 +387,7 @@
             orow[g, half, :] = pack_rows(whole).astype(BF16)
             ocol[half, :] = whole[:, CHUNK - EDGE :].astype(BF16)
         trail_row(g).start()
+        end_round(g)
         return 0
 
     lax.fori_loop(0, CHUNKS, chunk_step, 0)
@@ -551,6 +583,8 @@
             dma((9,)), dma((2 * CHUNKS + 4,)), dma((2 * CHUNKS + 4,)), dma((2,)), dma((2,)),
             dma((n_col,)), dma((n_col,)), dma((n_row // 2,)), dma((n_row // 2,)),
             dma((n_col,)), dma((n_col,)),
+            pltpu.SemaphoreType.REGULAR((CHUNKS,)), pltpu.SemaphoreType.REGULAR((CHUNKS,)),
+            pltpu.SemaphoreType.REGULAR,
         ],
         compiler_params=pltpu.CompilerParams(
             collective_id=1, has_side_effects=True, vmem_limit_bytes=60 * 1024 * 1024),

time: 65 us -> 64.6 us (level)
  no operation moved by 1% of the time
where the time goes in v4:
time: 64.6 us; the launch traced here: 64.4 us
  Pallas kernels  63.8 us (99%)
  between operations  0.65 us (1%)
    pallas_call x1, Pallas kernels, shards(): pl.pallas_call(functools.partial(block_kernel, n_row, n_col, spp, factor)...  61.4 us
    pallas_call x1, Pallas kernels, shards(): pl.pallas_call(finish_kernel, out_shape=outs, in_specs=[vmem] * 3, out_sp...  2.34 us

profile of v4, /device:TPU:1, one launch (start us, length us, event | category | flops | bytes accessed | tf_op | source)
XLA Modules:
  0.0 64.4 jit_solution(11605966064484013363)
XLA Ops:
  0.6 61.4 %shard_map.160 = (bf16[8,12288]{1,0:T(8,128)(2,1)}, bf16[8,12288]{1,0:T(8,128)(2,1)}, f32[208,768]{1,0:T(8,128)}) custom-call(bf16[8,12288]{1,0:T(8,128)(2,1)} %refs_0_.1, bf16[8,12288]{1,0:T(8,128)(2,1)} %refs_1_.1, bf16[192,576]{1,0:T(8,128)(2,1)} %refs_2_.1, f32[576]{0:T(1024)} %refs_3_.1, bf16[192,192]{1,0:T(8,128)(2,1)} %refs_4_.1, f32[192]{0:T(256)} %refs_5_.1, ...), custom_call_target="tpu_custom_call" | custom-call | tf_op jit(solution)/shard_map/pallas_call | solution.py:558
  62.1 2.3 %shard_map.161 = (bf16[8,12288]{1,0:T(8,128)(2,1)}, bf16[8,12288]{1,0:T(8,128)(2,1)}, f32[192,576]{1,0:T(8,128)}, f32[576]{0:T(1024)}, f32[192,192]{1,0:T(8,128)...) custom-call(bf16[8,12288]{1,0:T(8,128)(2,1)} %get-tuple-element.12.res, ...), custom_call_target="tpu_custom_call" | custom-call | tf_op jit(solution)/shard_map/pallas_call | solution.py:596

commit v5 on v4

--- a/solution.py
+++ b/solution.py
@@ -22,7 +22,7 @@
 WINDOWS = TILE_COLS // WIN
 SPAN = WIN * WIDTH
 TOKENS_HERE = WINDOWS * CELLS
-CHUNKS = 4
+CHUNKS = 2
 PER_CHUNK = WINDOWS // CHUNKS
 CHUNK_TOKENS = PER_CHUNK * CELLS
 CHUNK = PER_CHUNK * SPAN
@@ -188,7 +188,7 @@
      res, gin, total_out,
      img, cot, wqkv, bqkv, wproj, bproj, gain_ref, shift_ref, table_ref,
      irow, icol, hrow, hcol, hdiag, orow, ocol, rrow, rcol, rdiag,
-     field, cfield, corner, weights, xd, xhid, xatt, sums, gsum,
+     field, cfield, corner, weights, xs, cs, dh, xd, xhid, xatt, sums, gsum,
      bias, onehot, padded, diag, gs, c_out, c_in, plane_buf, p_in, z_out, z_in, half_buf, last_in,
      ls, hs, hr, cs_sem, cr_sem, ps, pr, zs, zr, as_sem, ar_sem,
      row_known, col_known, pair_known) = refs
@@ -225,7 +225,7 @@
                    (below, right)):
         greet(device)
 
-    rounds = [(g, 2**g) for g in range(CHUNKS)]
+    rounds = [(g, 2**g) for g in range(4)]
     row_rounds = [(g, d) for g, d in rounds if 4 * d <= n_row]
     col_rounds = [(g, d) for g, d in rounds if 4 * d <= n_col]
 
@@ -245,24 +245,17 @@
                 tell(col_known.at[k], (my_r, lax.rem(my_c + d, n_col)))
                 tell(col_known.at[k], (my_r, lax.rem(my_c + n_col - d, n_col)))
 
-        @pl.when(g == CHUNKS - 1)
+        @pl.when(g == 3)
         def _():
             tell(pair_known, (my_r + 1 - 2 * lax.rem(my_r, 2), my_c))
 
     def end_round(g):
-        for k, _ in row_rounds:
-            @pl.when(g == k)
-            def _():
-                pl.semaphore_wait(row_known.at[k], 2)
-
-        for k, _ in col_rounds:
-            @pl.when(g == k)
-            def _():
-                pl.semaphore_wait(col_known.at[k], 2)
-
-        @pl.when(g == CHUNKS - 1)
-        def _():
-            pl.semaphore_wait(pair_known, 1)
+        for known, known_rounds in ((row_known, row_rounds), (col_known, col_rounds)):
+            for k, _ in known_rounds:
+                if k < 3:
+                    @pl.when(g == k)
+                    def _():
+                        pl.semaphore_wait(known.at[k], 2)
 
     def remote(src, dst, send, recv, device):
         return pltpu.make_async_remote_copy(
@@ -298,6 +291,7 @@
         lead_row(g).start()
     for copy in lead:
         copy.start()
+    start_round(0)
 
     for copy in local[2:]:
         copy.wait()
@@ -326,7 +320,6 @@
         final = g == CHUNKS - 1
         lanes = pl.ds(pl.multiple_of(EDGE + g * CHUNK, 128), CHUNK)
         rows = pl.ds(pl.multiple_of(g * CHUNK_TOKENS, CHUNK_TOKENS), CHUNK_TOKENS)
-        start_round(g)
         lead_row(g).wait_recv()
         tokens = []
         for i, src in enumerate((field, cfield)):
@@ -357,7 +350,8 @@
             found.append(window_step(q[r], k[r], v[r], da[r], add, gsum))
         att, dq, dk, dv = [jnp.concatenate([part[i] for part in found], 0) for i in range(4)]
         xatt[rows, :] = att
-        out = x + dot(att, wproj[...]) + proj_bias
+        xs[rows, :] = x
+        cs[rows, :] = cot_f
         d_hidden = jnp.zeros((CHUNK_TOKENS, WIDTH), F32)
         for i, part in enumerate((dq, dk, dv)):
             part_b = part.astype(BF16)
@@ -368,6 +362,63 @@
         sums[3] += fold(cot_f)
         sums[4] += fold(d_hidden * normed)
         sums[5] += fold(d_hidden)
+        dh[rows, :] = d_hidden
+        end_round(g + 1)
+        start_round(g + 2)
+        return 0
+
+    end_round(0)
+    start_round(1)
+    lax.fori_loop(0, CHUNKS, chunk_step, 0)
+
+    hidden_t = xhid[...].T
+    for i in range(3):
+        gs[0:WIDTH, i * WIDTH : (i + 1) * WIDTH] = dot(hidden_t, xd[i])
+    gs[0:WIDTH, 3 * WIDTH :] = dot(xatt[...], xd[3], 0, 0)
+    for i in range(4):
+        gs[WIDTH : WIDTH + 1, i * WIDTH : (i + 1) * WIDTH] = jnp.sum(sums[i], 0, keepdims=True)
+    for i in range(2):
+        gs[WIDTH + 1 : WIDTH + 2, i * WIDTH : (i + 1) * WIDTH] = jnp.sum(
+            sums[4 + i], 0, keepdims=True)
+    for h, line in enumerate(table_grad(gsum[...], onehot, diag)):
+        gs[WIDTH + 2 + h : WIDTH + 3 + h, 0:256] = line
+
+    mine = pl.ds(pl.multiple_of(core * MID, 128), MID)
+    other = pl.ds(pl.multiple_of((1 - core) * MID, 128), MID)
+    partner = (my_r, my_c + 1 - 2 * core)
+    c_out[...] = gs[:, other].astype(BF16)
+    swap = remote(c_out, c_in, cs_sem.at[0], cr_sem.at[0], partner)
+    swap.start()
+    swap.wait_recv()
+    plane_buf[...] = (gs[:, mine] + c_in[...].astype(F32)).astype(BF16).reshape(
+        owners, rows_each, MID)
+
+    def scatter(p, slot):
+        return remote(plane_buf.at[p], p_in.at[slot], ps.at[p], pr.at[slot], plane_peer(p))
+
+    def from_plane(p):
+        return remote(plane_buf.at[0], p_in.at[p], ps.at[0], pr.at[p], plane_peer(p))
+
+    def send_scatter(k, _):
+        p = lax.rem(my_p + k, n_plane)
+
+        @pl.when(p < owners)
+        def _():
+            scatter(p, my_p).start()
+
+        return 0
+
+    pl.semaphore_wait(pair_known, 1)
+    lax.fori_loop(1, n_plane, send_scatter, 0)
+
+    def output_step(g, _):
+        lanes = pl.ds(pl.multiple_of(EDGE + g * CHUNK, 128), CHUNK)
+        rows = pl.ds(pl.multiple_of(g * CHUNK_TOKENS, CHUNK_TOKENS), CHUNK_TOKENS)
+        x, cot_f, d_hidden = xs[rows, :], cs[rows, :], dh[rows, :]
+        center = x - jnp.mean(x, 1, keepdims=True)
+        inv_std = lax.rsqrt(jnp.mean(center * center, 1, keepdims=True) + EPS)
+        normed = center * inv_std
+        out = x + dot(xatt[rows, :], wproj[...]) + proj_bias
         d_normed = d_hidden * gain
         d_tokens = cot_f + inv_std * (
             d_normed
@@ -387,51 +438,49 @@
             orow[g, half, :] = pack_rows(whole).astype(BF16)
             ocol[half, :] = whole[:, CHUNK - EDGE :].astype(BF16)
         trail_row(g).start()
-        end_round(g)
         return 0
 
-    lax.fori_loop(0, CHUNKS, chunk_step, 0)
+    lax.fori_loop(0, CHUNKS, output_step, 0)
     for copy in trail:
         copy.start()
 
-    hidden_t = xhid[...].T
-    for i in range(3):
-        gs[0:WIDTH, i * WIDTH : (i + 1) * WIDTH] = dot(hidden_t, xd[i])
-    gs[0:WIDTH, 3 * WIDTH :] = dot(xatt[...], xd[3], 0, 0)
-    for i in range(4):
-        gs[WIDTH : WIDTH + 1, i * WIDTH : (i + 1) * WIDTH] = jnp.sum(sums[i], 0, keepdims=True)
-    for i in range(2):
-        gs[WIDTH + 1 : WIDTH + 2, i * WIDTH : (i + 1) * WIDTH] = jnp.sum(
-            sums[4 + i], 0, keepdims=True)
-    for h, line in enumerate(table_grad(gsum[...], onehot, diag)):
-        gs[WIDTH + 2 + h : WIDTH + 3 + h, 0:256] = line
-
-    mine = pl.ds(pl.multiple_of(core * MID, 128), MID)
-    other = pl.ds(pl.multiple_of((1 - core) * MID, 128), MID)
-    partner = (my_r, my_c + 1 - 2 * core)
-    c_out[...] = gs[:, other].astype(BF16)
-    swap = remote(c_out, c_in, cs_sem.at[0], cr_sem.at[0], partner)
-    swap.start()
-    swap.wait_recv()
-    plane_buf[...] = (gs[:, mine] + c_in[...].astype(F32)).astype(BF16).reshape(
-        owners, rows_each, MID)
-
-    def scatter(p, slot):
-        return remote(plane_buf.at[p], p_in.at[slot], ps.at[p], pr.at[slot], plane_peer(p))
-
-    def from_plane(p):
-        return remote(plane_buf.at[0], p_in.at[p], ps.at[0], pr.at[p], plane_peer(p))
-
-    def send_scatter(k, _):
-        p = lax.rem(my_p + k, n_plane)
-
-        @pl.when(p < owners)
-        def _():
-            scatter(p, my_p).start()
-
-        return 0
-
-    lax.fori_loop(1, n_plane, send_scatter, 0)
+    def along_z(z, slot):
+        return remote(z_out, z_in.at[slot], zs.at[z], zr.at[slot], z_peer(z))
+
+    def spread(p, owner):
+        return remote(half_buf.at[owner], half_buf.at[owner], as_sem.at[p], ar_sem.at[owner],
+                      plane_peer(p))
+
+    def loop_plane(step):
+        def one(k, _):
+            step(lax.rem(my_p + k, n_plane))
+            return 0
+
+        lax.fori_loop(1, n_plane, one, 0)
+
+    def loop_z(step):
+        def one(k, _):
+            step(lax.rem(my_z + k, n_z))
+            return 0
+
+        lax.fori_loop(1, n_z, one, 0)
+
+    @pl.when(my_p < owners)
+    def _():
+        p_in[my_p] = plane_buf[my_p]
+        loop_plane(lambda p: from_plane(p).wait_recv())
+        acc = p_in[0].astype(F32)
+        for j in range(1, n_plane):
+            acc = acc + p_in[j].astype(F32)
+        z_out[...] = acc.astype(BF16)
+
+    if len(row_rounds) > 3:
+        pl.semaphore_wait(row_known.at[3], 2)
+
+    @pl.when(my_p < owners)
+    def _():
+        loop_z(lambda z: along_z(z, my_z).start())
+        z_in[my_z] = z_out[...]
 
     for g in range(CHUNKS):
         trail_row(g).wait_recv()
@@ -448,37 +497,8 @@
             whole = merge_rows(rrow[g, half, :].astype(F32), src[:, start : start + CHUNK])
             dst[:, start : start + size] = whole[:, :size].astype(BF16)
 
-    def along_z(z, slot):
-        return remote(z_out, z_in.at[slot], zs.at[z], zr.at[slot], z_peer(z))
-
-    def spread(p, owner):
-        return remote(half_buf.at[owner], half_buf.at[owner], as_sem.at[p], ar_sem.at[owner],
-                      plane_peer(p))
-
-    def loop_plane(step):
-        def one(k, _):
-            step(lax.rem(my_p + k, n_plane))
-            return 0
-
-        lax.fori_loop(1, n_plane, one, 0)
-
-    def loop_z(step):
-        def one(k, _):
-            step(lax.rem(my_z + k, n_z))
-            return 0
-
-        lax.fori_loop(1, n_z, one, 0)
-
     @pl.when(my_p < owners)
     def _():
-        p_in[my_p] = plane_buf[my_p]
-        loop_plane(lambda p: from_plane(p).wait_recv())
-        acc = p_in[0].astype(F32)
-        for j in range(1, n_plane):
-            acc = acc + p_in[j].astype(F32)
-        z_out[...] = acc.astype(BF16)
-        loop_z(lambda z: along_z(z, my_z).start())
-        z_in[my_z] = z_out[...]
         loop_z(lambda z: along_z(z, z).wait_recv())
         acc = z_in[0].astype(F32)
         for j in range(1, n_z):
@@ -566,6 +586,9 @@
             pltpu.VMEM((WIN, LANES + EDGE), F32), pltpu.VMEM((WIN, LANES + EDGE), F32),
             pltpu.VMEM((2, WIN, EDGE), F32),
             pltpu.VMEM((3, WIDTH, WIDTH), BF16),
+            pltpu.VMEM((TOKENS_HERE, WIDTH), F32),
+            pltpu.VMEM((TOKENS_HERE, WIDTH), F32),
+            pltpu.VMEM((TOKENS_HERE, WIDTH), F32),
             pltpu.VMEM((4, TOKENS_HERE, WIDTH), BF16),
             pltpu.VMEM((TOKENS_HERE, WIDTH), BF16),
             pltpu.VMEM((TOKENS_HERE, WIDTH), BF16),
@@ -583,7 +606,7 @@
             dma((9,)), dma((2 * CHUNKS + 4,)), dma((2 * CHUNKS + 4,)), dma((2,)), dma((2,)),
             dma((n_col,)), dma((n_col,)), dma((n_row // 2,)), dma((n_row // 2,)),
             dma((n_col,)), dma((n_col,)),
-            pltpu.SemaphoreType.REGULAR((CHUNKS,)), pltpu.SemaphoreType.REGULAR((CHUNKS,)),
+            pltpu.SemaphoreType.REGULAR((4,)), pltpu.SemaphoreType.REGULAR((4,)),
             pltpu.SemaphoreType.REGULAR,
         ],
         compiler_params=pltpu.CompilerParams(

time: 64.6 us -> 62 us (0.960)
  Pallas kernels: 63.8 us -> 61.2 us
    pallas_call x1, Pallas kernels: 61.4 us -> 58.8 us  [shards(): pl.pallas_call(functools.partial(block_kernel, n_row, n_col, spp, factor)...]
where the time goes in v5:
time: 62 us; the launch traced here: 61.8 us
  Pallas kernels  61.2 us (99%)
  between operations  0.65 us (1%)
    pallas_call x1, Pallas kernels, shards(): pl.pallas_call(functools.partial(block_kernel, n_row, n_col, spp, factor)...  58.8 us
    pallas_call x1, Pallas kernels, shards(): pl.pallas_call(finish_kernel, out_shape=outs, in_specs=[vmem] * 3, out_sp...  2.34 us

profile of v5, /device:TPU:1, one launch (start us, length us, event | category | flops | bytes accessed | tf_op | source)
XLA Modules:
  0.0 61.8 jit_solution(15342131779796509952)
XLA Ops:
  0.6 58.8 %shard_map.160 = (bf16[8,12288]{1,0:T(8,128)(2,1)}, bf16[8,12288]{1,0:T(8,128)(2,1)}, f32[208,768]{1,0:T(8,128)}) custom-call(bf16[8,12288]{1,0:T(8,128)(2,1)} %refs_0_.1, bf16[8,12288]{1,0:T(8,128)(2,1)} %refs_1_.1, bf16[192,576]{1,0:T(8,128)(2,1)} %refs_2_.1, f32[576]{0:T(1024)} %refs_3_.1, bf16[192,192]{1,0:T(8,128)(2,1)} %refs_4_.1, f32[192]{0:T(256)} %refs_5_.1, ...), custom_call_target="tpu_custom_call" | custom-call | tf_op jit(solution)/shard_map/pallas_call | solution.py:578
  59.5 2.3 %shard_map.161 = (bf16[8,12288]{1,0:T(8,128)(2,1)}, bf16[8,12288]{1,0:T(8,128)(2,1)}, f32[192,576]{1,0:T(8,128)}, f32[576]{0:T(1024)}, f32[192,192]{1,0:T(8,128)...) custom-call(bf16[8,12288]{1,0:T(8,128)(2,1)} %get-tuple-element.12.res, ...), custom_call_target="tpu_custom_call" | custom-call | tf_op jit(solution)/shard_map/pallas_call | solution.py:619

commit v6 on v5

--- a/solution.py
+++ b/solution.py
@@ -23,6 +23,7 @@
 SPAN = WIN * WIDTH
 TOKENS_HERE = WINDOWS * CELLS
 CHUNKS = 2
+LOOSE = False
 PER_CHUNK = WINDOWS // CHUNKS
 CHUNK_TOKENS = PER_CHUNK * CELLS
 CHUNK = PER_CHUNK * SPAN
@@ -393,23 +394,49 @@
     plane_buf[...] = (gs[:, mine] + c_in[...].astype(F32)).astype(BF16).reshape(
         owners, rows_each, MID)
 
-    def scatter(p, slot):
-        return remote(plane_buf.at[p], p_in.at[slot], ps.at[p], pr.at[slot], plane_peer(p))
-
-    def from_plane(p):
-        return remote(plane_buf.at[0], p_in.at[p], ps.at[0], pr.at[p], plane_peer(p))
-
-    def send_scatter(k, _):
-        p = lax.rem(my_p + k, n_plane)
-
+    def loop_group(me, count, step):
+        def one(k, _):
+            step(lax.rem(me + k, count))
+            return 0
+
+        lax.fori_loop(1, count, one, 0, unroll=LOOSE)
+
+    def loop_plane(step):
+        loop_group(my_p, n_plane, step)
+
+    def loop_z(step):
+        loop_group(my_z, n_z, step)
+
+    def stage_of(buffer, count, send, recv):
+        part = buffer.at[pl.ds(0, count)]
+        return remote(part, part, send, recv, partner)
+
+    def from_all_owners(step):
+        @pl.when(my_p < owners)
+        def _():
+            step(owners - 1)
+
+        @pl.when(my_p >= owners)
+        def _():
+            step(owners)
+
+    def scatter(p):
+        return remote(plane_buf.at[p], p_in.at[my_p], ps.at[0], pr.at[0], plane_peer(p))
+
+    def along_z(z):
+        return remote(z_out.at[0], z_in.at[my_z], zs.at[0], zr.at[0], z_peer(z))
+
+    def spread(p):
+        return remote(half_buf.at[my_p], half_buf.at[my_p], as_sem.at[0], ar_sem.at[0],
+                      plane_peer(p))
+
+    def send_scatter(p):
         @pl.when(p < owners)
         def _():
-            scatter(p, my_p).start()
-
-        return 0
+            scatter(p).start()
 
     pl.semaphore_wait(pair_known, 1)
-    lax.fori_loop(1, n_plane, send_scatter, 0)
+    loop_plane(send_scatter)
 
     def output_step(g, _):
         lanes = pl.ds(pl.multiple_of(EDGE + g * CHUNK, 128), CHUNK)
@@ -444,43 +471,22 @@
     for copy in trail:
         copy.start()
 
-    def along_z(z, slot):
-        return remote(z_out, z_in.at[slot], zs.at[z], zr.at[slot], z_peer(z))
-
-    def spread(p, owner):
-        return remote(half_buf.at[owner], half_buf.at[owner], as_sem.at[p], ar_sem.at[owner],
-                      plane_peer(p))
-
-    def loop_plane(step):
-        def one(k, _):
-            step(lax.rem(my_p + k, n_plane))
-            return 0
-
-        lax.fori_loop(1, n_plane, one, 0)
-
-    def loop_z(step):
-        def one(k, _):
-            step(lax.rem(my_z + k, n_z))
-            return 0
-
-        lax.fori_loop(1, n_z, one, 0)
+    def total_of(buffer, count):
+        acc = buffer[0].astype(F32)
+        for j in range(1, count):
+            acc = acc + buffer[j].astype(F32)
+        return acc
+
+    if len(row_rounds) > 3:
+        pl.semaphore_wait(row_known.at[3], 2)
 
     @pl.when(my_p < owners)
     def _():
         p_in[my_p] = plane_buf[my_p]
-        loop_plane(lambda p: from_plane(p).wait_recv())
-        acc = p_in[0].astype(F32)
-        for j in range(1, n_plane):
-            acc = acc + p_in[j].astype(F32)
-        z_out[...] = acc.astype(BF16)
-
-    if len(row_rounds) > 3:
-        pl.semaphore_wait(row_known.at[3], 2)
-
-    @pl.when(my_p < owners)
-    def _():
-        loop_z(lambda z: along_z(z, my_z).start())
-        z_in[my_z] = z_out[...]
+        stage_of(p_in, n_plane - 1, ps.at[0], pr.at[0]).wait_recv()
+        z_out[0] = total_of(p_in, n_plane).astype(BF16)
+        loop_z(lambda z: along_z(z).start())
+        z_in[my_z] = z_out[0]
 
     for g in range(CHUNKS):
         trail_row(g).wait_recv()
@@ -499,19 +505,12 @@
 
     @pl.when(my_p < owners)
     def _():
-        loop_z(lambda z: along_z(z, z).wait_recv())
-        acc = z_in[0].astype(F32)
-        for j in range(1, n_z):
-            acc = acc + z_in[j].astype(F32)
-        half_buf[my_p] = acc.astype(BF16)
-        loop_plane(lambda p: spread(p, my_p).start())
-
-    def arrive(p):
-        @pl.when(p < owners)
-        def _():
-            spread(p, p).wait_recv()
-
-    loop_plane(arrive)
+        stage_of(z_in, n_z - 1, zs.at[0], zr.at[0]).wait_recv()
+        half_buf[my_p] = total_of(z_in, n_z).astype(BF16)
+        loop_plane(lambda p: spread(p).start())
+
+    from_all_owners(
+        lambda count: stage_of(half_buf, count, as_sem.at[0], ar_sem.at[0]).wait_recv())
     back = remote(half_buf, last_in, cs_sem.at[1], cr_sem.at[1], partner)
     back.start()
     flat = (owners * rows_each, MID)
@@ -525,17 +524,12 @@
     for copy in lead + trail + (swap, back):
         copy.wait_send()
 
-    def sent(p):
-        @pl.when(p < owners)
-        def _():
-            scatter(p, my_p).wait_send()
-
-    loop_plane(sent)
+    from_all_owners(lambda count: stage_of(plane_buf, count, ps.at[0], pr.at[0]).wait_send())
 
     @pl.when(my_p < owners)
     def _():
-        loop_z(lambda z: along_z(z, my_z).wait_send())
-        loop_plane(lambda p: spread(p, my_p).wait_send())
+        stage_of(z_in, n_z - 1, zs.at[0], zr.at[0]).wait_send()
+        stage_of(p_in, n_plane - 1, as_sem.at[0], ar_sem.at[0]).wait_send()
 
 
 def finish_kernel(res, gin, total, *refs):
@@ -601,11 +595,10 @@
             pltpu.VMEM((owners * rows_each, WIDE), F32),
             pltpu.VMEM(half, BF16), pltpu.VMEM(half, BF16),
             pltpu.VMEM(halves, BF16), pltpu.VMEM((n_col,) + stripe, BF16),
-            pltpu.VMEM(stripe, BF16), pltpu.VMEM((n_row // 2,) + stripe, BF16),
+            pltpu.VMEM((1,) + stripe, BF16), pltpu.VMEM((n_row // 2,) + stripe, BF16),
             pltpu.VMEM(halves, BF16), pltpu.VMEM(halves, BF16),
             dma((9,)), dma((2 * CHUNKS + 4,)), dma((2 * CHUNKS + 4,)), dma((2,)), dma((2,)),
-            dma((n_col,)), dma((n_col,)), dma((n_row // 2,)), dma((n_row // 2,)),
-            dma((n_col,)), dma((n_col,)),
+            dma((1,)), dma((1,)), dma((1,)), dma((1,)), dma((1,)), dma((1,)),
             pltpu.SemaphoreType.REGULAR((4,)), pltpu.SemaphoreType.REGULAR((4,)),
             pltpu.SemaphoreType.REGULAR,
         ],

time: 62 us -> 60.6 us (0.977)
  Pallas kernels: 61.2 us -> 59.8 us
    pallas_call x1, Pallas kernels: 58.8 us -> 57.4 us  [shards(): pl.pallas_call(functools.partial(block_kernel, n_row, n_col, spp, factor)...]
where the time goes in v6:
time: 60.6 us; the launch traced here: 60.4 us
  Pallas kernels  59.8 us (99%)
  between operations  0.65 us (1%)
    pallas_call x1, Pallas kernels, shards(): pl.pallas_call(functools.partial(block_kernel, n_row, n_col, spp, factor)...  57.4 us
    pallas_call x1, Pallas kernels, shards(): pl.pallas_call(finish_kernel, out_shape=outs, in_specs=[vmem] * 3, out_sp...  2.34 us

profile of v6, /device:TPU:1, one launch (start us, length us, event | category | flops | bytes accessed | tf_op | source)
XLA Modules:
  0.0 60.4 jit_solution(15913773951513725436)
XLA Ops:
  0.6 57.4 %shard_map.160 = (bf16[8,12288]{1,0:T(8,128)(2,1)}, bf16[8,12288]{1,0:T(8,128)(2,1)}, f32[208,768]{1,0:T(8,128)}) custom-call(bf16[8,12288]{1,0:T(8,128)(2,1)} %refs_0_.1, bf16[8,12288]{1,0:T(8,128)(2,1)} %refs_1_.1, bf16[192,576]{1,0:T(8,128)(2,1)} %refs_2_.1, f32[576]{0:T(1024)} %refs_3_.1, bf16[192,192]{1,0:T(8,128)(2,1)} %refs_4_.1, f32[192]{0:T(256)} %refs_5_.1, ...), custom_call_target="tpu_custom_call" | custom-call | tf_op jit(solution)/shard_map/pallas_call | solution.py:572
  58.1 2.3 %shard_map.161 = (bf16[8,12288]{1,0:T(8,128)(2,1)}, bf16[8,12288]{1,0:T(8,128)(2,1)}, f32[192,576]{1,0:T(8,128)}, f32[576]{0:T(1024)}, f32[192,192]{1,0:T(8,128)...) custom-call(bf16[8,12288]{1,0:T(8,128)(2,1)} %get-tuple-element.12.res, ...), custom_call_target="tpu_custom_call" | custom-call | tf_op jit(solution)/shard_map/pallas_call | solution.py:612

commit v7 on v6

--- a/solution.py
+++ b/solution.py
@@ -278,18 +278,20 @@
 
     local[0].wait()
     local[1].wait()
-    for i, (src, dst) in enumerate(((img, field), (cot, cfield))):
-        half = slice(i * WIN, i * WIN + WIN)
-        tile = src[...].astype(F32)
-        icol[half, :] = tile[:, :EDGE].astype(BF16)
-        dst[:, :LANES] = tile
-        dst[:, LANES:] = tile[:, :EDGE]
-        for g in range(CHUNKS):
-            lanes = slice(EDGE + g * CHUNK, EDGE + (g + 1) * CHUNK)
-            irow[g, half, :] = pack_rows(dst[:, lanes]).astype(BF16)
     pl.semaphore_wait(barrier, 6)
     for g in range(CHUNKS):
+        start = EDGE + g * CHUNK
+        size = min(CHUNK, LANES - start)
+        for i, (src, dst) in enumerate(((img, field), (cot, cfield))):
+            half = slice(i * WIN, i * WIN + WIN)
+            tile = src[:, start : start + size].astype(F32)
+            if size < CHUNK:
+                tile = jnp.concatenate([tile, src[:, :EDGE].astype(F32)], 1)
+            dst[:, start : start + CHUNK] = tile
+            irow[g, half, :] = pack_rows(tile).astype(BF16)
         lead_row(g).start()
+    for i, src in enumerate((img, cot)):
+        icol[i * WIN : i * WIN + WIN, :] = src[:, :EDGE]
     for copy in lead:
         copy.start()
     start_round(0)
@@ -301,6 +303,7 @@
     build_bias(table_ref, onehot, padded, diag, bias, last_row, last_col)
     gsum[...] = jnp.zeros_like(gsum)
     sums[...] = jnp.zeros_like(sums)
+    corner[...] = jnp.zeros_like(corner)
     gs[WIDTH:, :] = jnp.zeros((owners * rows_each - WIDTH, WIDE), F32)
     for i in range(3):
         weights[i] = wqkv[:, i * WIDTH : (i + 1) * WIDTH]
@@ -310,18 +313,21 @@
     gain = gain_ref[...].reshape(1, WIDTH)
     shift = shift_ref[...].reshape(1, WIDTH)
 
-    for copy in lead:
-        copy.wait_recv()
-    for i in range(2):
-        half = slice(i * WIN, i * WIN + WIN)
-        corner[i] = jnp.where(
-            upper((WIN, EDGE)), hdiag[half, :].astype(F32), hcol[half, :].astype(F32))
-
     def chunk_step(g, _):
         final = g == CHUNKS - 1
         lanes = pl.ds(pl.multiple_of(EDGE + g * CHUNK, 128), CHUNK)
         rows = pl.ds(pl.multiple_of(g * CHUNK_TOKENS, CHUNK_TOKENS), CHUNK_TOKENS)
         lead_row(g).wait_recv()
+
+        @pl.when(final)
+        def _():
+            for copy in lead:
+                copy.wait_recv()
+            for i in range(2):
+                half = slice(i * WIN, i * WIN + WIN)
+                corner[i] = jnp.where(
+                    upper((WIN, EDGE)), hdiag[half, :].astype(F32), hcol[half, :].astype(F32))
+
         tokens = []
         for i, src in enumerate((field, cfield)):
             half = slice(i * WIN, i * WIN + WIN)
@@ -467,9 +473,6 @@
         trail_row(g).start()
         return 0
 
-    lax.fori_loop(0, CHUNKS, output_step, 0)
-    for copy in trail:
-        copy.start()
 
     def total_of(buffer, count):
         acc = buffer[0].astype(F32)
@@ -487,6 +490,16 @@
         z_out[0] = total_of(p_in, n_plane).astype(BF16)
         loop_z(lambda z: along_z(z).start())
         z_in[my_z] = z_out[0]
+
+    lax.fori_loop(0, CHUNKS, output_step, 0)
+    for copy in trail:
+        copy.start()
+
+    @pl.when(my_p < owners)
+    def _():
+        stage_of(z_in, n_z - 1, zs.at[0], zr.at[0]).wait_recv()
+        half_buf[my_p] = total_of(z_in, n_z).astype(BF16)
+        loop_plane(lambda p: spread(p).start())
 
     for g in range(CHUNKS):
         trail_row(g).wait_recv()
@@ -503,12 +516,6 @@
             whole = merge_rows(rrow[g, half, :].astype(F32), src[:, start : start + CHUNK])
             dst[:, start : start + size] = whole[:, :size].astype(BF16)
 
-    @pl.when(my_p < owners)
-    def _():
-        stage_of(z_in, n_z - 1, zs.at[0], zr.at[0]).wait_recv()
-        half_buf[my_p] = total_of(z_in, n_z).astype(BF16)
-        loop_plane(lambda p: spread(p).start())
-
     from_all_owners(
         lambda count: stage_of(half_buf, count, as_sem.at[0], ar_sem.at[0]).wait_recv())
     back = remote(half_buf, last_in, cs_sem.at[1], cr_sem.at[1], partner)
@@ -534,19 +541,23 @@
 
 def finish_kernel(res, gin, total, *refs):
     outs, (b0, b1, w0, w1, v0, v1, v2, t0, sems) = refs[:9], refs[9:]
+    staged = (res, gin, w0, b0, w1, v0, v1, v2, t0)
+    copies = [
+        pltpu.make_async_copy(src, dst, sems.at[i]) for i, (src, dst) in enumerate(zip(staged, outs))
+    ]
+    for copy in copies[:2]:
+        copy.start()
     w0[...] = total[0:WIDTH, : 3 * WIDTH]
+    copies[2].start()
     w1[...] = total[0:WIDTH, 3 * WIDTH :]
+    copies[4].start()
     b0[...] = total[WIDTH : WIDTH + 1, : 3 * WIDTH].reshape(3 * WIDTH)
     v0[...] = total[WIDTH : WIDTH + 1, 3 * WIDTH :].reshape(WIDTH)
     v1[...] = total[WIDTH + 1 : WIDTH + 2, :WIDTH].reshape(WIDTH)
     v2[...] = total[WIDTH + 1 : WIDTH + 2, WIDTH : 2 * WIDTH].reshape(WIDTH)
     t0[...] = total[WIDTH + 2 : WIDTH + 2 + HEADS, :RELS]
-    copies = [
-        pltpu.make_async_copy(src, dst, sems.at[i])
-        for i, (src, dst) in enumerate(zip((res, gin, w0, b0, w1, v0, v1, v2, t0), outs))
-    ]
-    for copy in copies:
-        copy.start()
+    for i in (3, 5, 6, 7, 8):
+        copies[i].start()
     for copy in copies:
         copy.wait()
 

time: 60.6 us -> 58 us (0.957)
  Pallas kernels: 59.8 us -> 57.2 us
    pallas_call x1, Pallas kernels: 57.4 us -> 54.9 us  [shards(): pl.pallas_call(functools.partial(block_kernel, n_row, n_col, spp, factor)...]
where the time goes in v7:
time: 58 us; the launch traced here: 57.9 us
  Pallas kernels  57.2 us (99%)
  between operations  0.65 us (1%)
    pallas_call x1, Pallas kernels, shards(): pl.pallas_call(functools.partial(block_kernel, n_row, n_col, spp, factor)...  54.9 us
    pallas_call x1, Pallas kernels, shards(): pl.pallas_call(finish_kernel, out_shape=outs, in_specs=[vmem] * 3, out_sp...  2.34 us

profile of v7, /device:TPU:1, one launch (start us, length us, event | category | flops | bytes accessed | tf_op | source)
XLA Modules:
  0.0 57.9 jit_solution(9631795360032383804)
XLA Ops:
  0.6 54.9 %shard_map.160 = (bf16[8,12288]{1,0:T(8,128)(2,1)}, bf16[8,12288]{1,0:T(8,128)(2,1)}, f32[208,768]{1,0:T(8,128)}) custom-call(bf16[8,12288]{1,0:T(8,128)(2,1)} %refs_0_.1, bf16[8,12288]{1,0:T(8,128)(2,1)} %refs_1_.1, bf16[192,576]{1,0:T(8,128)(2,1)} %refs_2_.1, f32[576]{0:T(1024)} %refs_3_.1, bf16[192,192]{1,0:T(8,128)(2,1)} %refs_4_.1, f32[192]{0:T(256)} %refs_5_.1, ...), custom_call_target="tpu_custom_call" | custom-call | tf_op jit(solution)/shard_map/pallas_call | solution.py:583
  55.5 2.3 %shard_map.161 = (bf16[8,12288]{1,0:T(8,128)(2,1)}, bf16[8,12288]{1,0:T(8,128)(2,1)}, f32[192,576]{1,0:T(8,128)}, f32[576]{0:T(1024)}, f32[192,192]{1,0:T(8,128)...) custom-call(bf16[8,12288]{1,0:T(8,128)(2,1)} %get-tuple-element.12.res, ...), custom_call_target="tpu_custom_call" | custom-call | tf_op jit(solution)/shard_map/pallas_call | solution.py:623

commit v8 on v7

--- a/solution.py
+++ b/solution.py
@@ -33,6 +33,7 @@
 STRIPES = 13
 WIDE = 4 * WIDTH
 MID = WIDE // 2
+PARTS = MID // 128
 
 MESH = pl.DeviceIdType.MESH
 F32 = jnp.float32
@@ -397,8 +398,9 @@
     swap = remote(c_out, c_in, cs_sem.at[0], cr_sem.at[0], partner)
     swap.start()
     swap.wait_recv()
-    plane_buf[...] = (gs[:, mine] + c_in[...].astype(F32)).astype(BF16).reshape(
-        owners, rows_each, MID)
+    halves = (gs[:, mine] + c_in[...].astype(F32)).astype(BF16)
+    for t in range(PARTS):
+        plane_buf[t] = halves[:, t * 128 : (t + 1) * 128].reshape(owners, rows_each, 128)
 
     def loop_group(me, count, step):
         def one(k, _):
@@ -413,9 +415,9 @@
     def loop_z(step):
         loop_group(my_z, n_z, step)
 
-    def stage_of(buffer, count, send, recv):
-        part = buffer.at[pl.ds(0, count)]
-        return remote(part, part, send, recv, partner)
+    def stage_of(buffer, t, count, send, recv):
+        part = buffer.at[t, pl.ds(0, count)]
+        return remote(part, part, send.at[t], recv.at[t], partner)
 
     def from_all_owners(step):
         @pl.when(my_p < owners)
@@ -426,23 +428,30 @@
         def _():
             step(owners)
 
-    def scatter(p):
-        return remote(plane_buf.at[p], p_in.at[my_p], ps.at[0], pr.at[0], plane_peer(p))
-
-    def along_z(z):
-        return remote(z_out.at[0], z_in.at[my_z], zs.at[0], zr.at[0], z_peer(z))
-
-    def spread(p):
-        return remote(half_buf.at[my_p], half_buf.at[my_p], as_sem.at[0], ar_sem.at[0],
+    def scatter(t, p):
+        return remote(plane_buf.at[t, p], p_in.at[t, my_p], ps.at[t], pr.at[t], plane_peer(p))
+
+    def along_z(t, z):
+        return remote(z_out.at[t], z_in.at[t, my_z], zs.at[t], zr.at[t], z_peer(z))
+
+    def spread(t, p):
+        return remote(half_buf.at[t, my_p], half_buf.at[t, my_p], as_sem.at[t], ar_sem.at[t],
                       plane_peer(p))
 
-    def send_scatter(p):
-        @pl.when(p < owners)
-        def _():
-            scatter(p).start()
+    def back(t):
+        return remote(half_buf.at[t], last_in.at[t], cs_sem.at[1 + t], cr_sem.at[1 + t], partner)
+
+    def send_scatter(t):
+        def one(p):
+            @pl.when(p < owners)
+            def _():
+                scatter(t, p).start()
+
+        loop_plane(one)
 
     pl.semaphore_wait(pair_known, 1)
-    loop_plane(send_scatter)
+    for t in range(PARTS):
+        send_scatter(t)
 
     def output_step(g, _):
         lanes = pl.ds(pl.multiple_of(EDGE + g * CHUNK, 128), CHUNK)
@@ -474,22 +483,23 @@
         return 0
 
 
-    def total_of(buffer, count):
-        acc = buffer[0].astype(F32)
+    def total_of(buffer, t, count):
+        acc = buffer[t, 0].astype(F32)
         for j in range(1, count):
-            acc = acc + buffer[j].astype(F32)
-        return acc
+            acc = acc + buffer[t, j].astype(F32)
+        return acc.astype(BF16)
 
     if len(row_rounds) > 3:
         pl.semaphore_wait(row_known.at[3], 2)
 
     @pl.when(my_p < owners)
     def _():
-        p_in[my_p] = plane_buf[my_p]
-        stage_of(p_in, n_plane - 1, ps.at[0], pr.at[0]).wait_recv()
-        z_out[0] = total_of(p_in, n_plane).astype(BF16)
-        loop_z(lambda z: along_z(z).start())
-        z_in[my_z] = z_out[0]
+        for t in range(PARTS):
+            p_in[t, my_p] = plane_buf[t, my_p]
+            stage_of(p_in, t, n_plane - 1, ps, pr).wait_recv()
+            z_out[t] = total_of(p_in, t, n_plane)
+            loop_z(lambda z: along_z(t, z).start())
+            z_in[t, my_z] = z_out[t]
 
     lax.fori_loop(0, CHUNKS, output_step, 0)
     for copy in trail:
@@ -497,9 +507,10 @@
 
     @pl.when(my_p < owners)
     def _():
-        stage_of(z_in, n_z - 1, zs.at[0], zr.at[0]).wait_recv()
-        half_buf[my_p] = total_of(z_in, n_z).astype(BF16)
-        loop_plane(lambda p: spread(p).start())
+        for t in range(PARTS):
+            stage_of(z_in, t, n_z - 1, zs, zr).wait_recv()
+            half_buf[t, my_p] = total_of(z_in, t, n_z)
+            loop_plane(lambda p: spread(t, p).start())
 
     for g in range(CHUNKS):
         trail_row(g).wait_recv()
@@ -516,27 +527,31 @@
             whole = merge_rows(rrow[g, half, :].astype(F32), src[:, start : start + CHUNK])
             dst[:, start : start + size] = whole[:, :size].astype(BF16)
 
-    from_all_owners(
-        lambda count: stage_of(half_buf, count, as_sem.at[0], ar_sem.at[0]).wait_recv())
-    back = remote(half_buf, last_in, cs_sem.at[1], cr_sem.at[1], partner)
-    back.start()
-    flat = (owners * rows_each, MID)
-    total_out[:, mine] = half_buf[...].astype(F32).reshape(flat) * grad_scale
-    back.wait_recv()
-    total_out[:, other] = last_in[...].astype(F32).reshape(flat) * grad_scale
+    def lanes_of(first, t):
+        return pl.ds(pl.multiple_of(first * MID + t * 128, 128), 128)
+
+    flat = (owners * rows_each, 128)
+    for t in range(PARTS):
+        from_all_owners(lambda count: stage_of(half_buf, t, count, as_sem, ar_sem).wait_recv())
+        back(t).start()
+        total_out[:, lanes_of(core, t)] = half_buf[t].astype(F32).reshape(flat) * grad_scale
+    for t in range(PARTS):
+        back(t).wait_recv()
+        total_out[:, lanes_of(1 - core, t)] = last_in[t].astype(F32).reshape(flat) * grad_scale
 
     for g in range(CHUNKS):
         lead_row(g).wait_send()
         trail_row(g).wait_send()
-    for copy in lead + trail + (swap, back):
+    for copy in lead + trail + (swap,):
         copy.wait_send()
-
-    from_all_owners(lambda count: stage_of(plane_buf, count, ps.at[0], pr.at[0]).wait_send())
-
-    @pl.when(my_p < owners)
-    def _():
-        stage_of(z_in, n_z - 1, zs.at[0], zr.at[0]).wait_send()
-        stage_of(p_in, n_plane - 1, as_sem.at[0], ar_sem.at[0]).wait_send()
+    for t in range(PARTS):
+        back(t).wait_send()
+        from_all_owners(lambda count: stage_of(plane_buf, t, count, ps, pr).wait_send())
+
+        @pl.when(my_p < owners)
+        def _():
+            stage_of(z_in, t, n_z - 1, zs, zr).wait_send()
+            stage_of(p_in, t, n_plane - 1, as_sem, ar_sem).wait_send()
 
 
 def finish_kernel(res, gin, total, *refs):
@@ -578,8 +593,8 @@
     row_halo = pltpu.VMEM((CHUNKS, 16, HALF), BF16)
     col_halo = pltpu.VMEM((16, EDGE), BF16)
     half = (owners * rows_each, MID)
-    halves = (owners, rows_each, MID)
-    stripe = (rows_each, MID)
+    stripe = (rows_each, 128)
+    halves = (PARTS, owners) + stripe
     parts = pl.pallas_call(
         functools.partial(block_kernel, n_row, n_col, spp, factor),
         out_shape=(tile, tile, jax.ShapeDtypeStruct((owners * rows_each, WIDE), F32)),
@@ -605,11 +620,12 @@
             pltpu.VMEM((HEADS, WIN, 128), F32),
             pltpu.VMEM((owners * rows_each, WIDE), F32),
             pltpu.VMEM(half, BF16), pltpu.VMEM(half, BF16),
-            pltpu.VMEM(halves, BF16), pltpu.VMEM((n_col,) + stripe, BF16),
-            pltpu.VMEM((1,) + stripe, BF16), pltpu.VMEM((n_row // 2,) + stripe, BF16),
+            pltpu.VMEM(halves, BF16), pltpu.VMEM((PARTS, n_col) + stripe, BF16),
+            pltpu.VMEM((PARTS,) + stripe, BF16), pltpu.VMEM((PARTS, n_row // 2) + stripe, BF16),
             pltpu.VMEM(halves, BF16), pltpu.VMEM(halves, BF16),
-            dma((9,)), dma((2 * CHUNKS + 4,)), dma((2 * CHUNKS + 4,)), dma((2,)), dma((2,)),
-            dma((1,)), dma((1,)), dma((1,)), dma((1,)), dma((1,)), dma((1,)),
+            dma((9,)), dma((2 * CHUNKS + 4,)), dma((2 * CHUNKS + 4,)), dma((1 + PARTS,)),
+            dma((1 + PARTS,)), dma((PARTS,)), dma((PARTS,)), dma((PARTS,)), dma((PARTS,)),
+            dma((PARTS,)), dma((PARTS,)),
             pltpu.SemaphoreType.REGULAR((4,)), pltpu.SemaphoreType.REGULAR((4,)),
             pltpu.SemaphoreType.REGULAR,
         ],

time: 58 us -> 57.1 us (0.984)
  Pallas kernels: 57.2 us -> 56.3 us
    pallas_call x1, Pallas kernels: 54.9 us -> 54 us  [shards(): pl.pallas_call(functools.partial(block_kernel, n_row, n_col, spp, factor)...]
where the time goes in v8:
time: 57.1 us; the launch traced here: 57 us
  Pallas kernels  56.3 us (99%)
  between operations  0.65 us (1%)
    pallas_call x1, Pallas kernels, shards(): pl.pallas_call(functools.partial(block_kernel, n_row, n_col, spp, factor)...  54 us
    pallas_call x1, Pallas kernels, shards(): pl.pallas_call(finish_kernel, out_shape=outs, in_specs=[vmem] * 3, out_sp...  2.34 us

profile of v8, /device:TPU:1, one launch (start us, length us, event | category | flops | bytes accessed | tf_op | source)
XLA Modules:
  0.0 57.0 jit_solution(2786342459439294845)
XLA Ops:
  0.6 54.0 %shard_map.160 = (bf16[8,12288]{1,0:T(8,128)(2,1)}, bf16[8,12288]{1,0:T(8,128)(2,1)}, f32[208,768]{1,0:T(8,128)}) custom-call(bf16[8,12288]{1,0:T(8,128)(2,1)} %refs_0_.1, bf16[8,12288]{1,0:T(8,128)(2,1)} %refs_1_.1, bf16[192,576]{1,0:T(8,128)(2,1)} %refs_2_.1, f32[576]{0:T(1024)} %refs_3_.1, bf16[192,192]{1,0:T(8,128)(2,1)} %refs_4_.1, f32[192]{0:T(256)} %refs_5_.1, ...), custom_call_target="tpu_custom_call" | custom-call | tf_op jit(solution)/shard_map/pallas_call | solution.py:598
  54.6 2.3 %shard_map.161 = (bf16[8,12288]{1,0:T(8,128)(2,1)}, bf16[8,12288]{1,0:T(8,128)(2,1)}, f32[192,576]{1,0:T(8,128)}, f32[576]{0:T(1024)}, f32[192,192]{1,0:T(8,128)...) custom-call(bf16[8,12288]{1,0:T(8,128)(2,1)} %get-tuple-element.12.res, ...), custom_call_target="tpu_custom_call" | custom-call | tf_op jit(solution)/shard_map/pallas_call | solution.py:639

commit v9 on v8

--- a/solution.py
+++ b/solution.py
@@ -22,7 +22,7 @@
 WINDOWS = TILE_COLS // WIN
 SPAN = WIN * WIDTH
 TOKENS_HERE = WINDOWS * CELLS
-CHUNKS = 2
+CHUNKS = 4
 LOOSE = False
 PER_CHUNK = WINDOWS // CHUNKS
 CHUNK_TOKENS = PER_CHUNK * CELLS
@@ -391,16 +391,16 @@
     for h, line in enumerate(table_grad(gsum[...], onehot, diag)):
         gs[WIDTH + 2 + h : WIDTH + 3 + h, 0:256] = line
 
-    mine = pl.ds(pl.multiple_of(core * MID, 128), MID)
-    other = pl.ds(pl.multiple_of((1 - core) * MID, 128), MID)
     partner = (my_r, my_c + 1 - 2 * core)
-    c_out[...] = gs[:, other].astype(BF16)
-    swap = remote(c_out, c_in, cs_sem.at[0], cr_sem.at[0], partner)
-    swap.start()
-    swap.wait_recv()
-    halves = (gs[:, mine] + c_in[...].astype(F32)).astype(BF16)
+
+    def lanes_of(first, t):
+        return pl.ds(pl.multiple_of(first * MID + t * 128, 128), 128)
+
+    swaps = [remote(c_out.at[t], c_in.at[t], cs_sem.at[PARTS + t], cr_sem.at[PARTS + t], partner)
+             for t in range(PARTS)]
     for t in range(PARTS):
-        plane_buf[t] = halves[:, t * 128 : (t + 1) * 128].reshape(owners, rows_each, 128)
+        c_out[t] = gs[:, lanes_of(1 - core, t)].astype(BF16)
+        swaps[t].start()
 
     def loop_group(me, count, step):
         def one(k, _):
@@ -439,7 +439,7 @@
                       plane_peer(p))
 
     def back(t):
-        return remote(half_buf.at[t], last_in.at[t], cs_sem.at[1 + t], cr_sem.at[1 + t], partner)
+        return remote(half_buf.at[t], last_in.at[t], cs_sem.at[t], cr_sem.at[t], partner)
 
     def send_scatter(t):
         def one(p):
@@ -451,6 +451,9 @@
 
     pl.semaphore_wait(pair_known, 1)
     for t in range(PARTS):
+        swaps[t].wait_recv()
+        part = (gs[:, lanes_of(core, t)] + c_in[t].astype(F32)).astype(BF16)
+        plane_buf[t] = part.reshape(owners, rows_each, 128)
         send_scatter(t)
 
     def output_step(g, _):
@@ -527,9 +530,6 @@
             whole = merge_rows(rrow[g, half, :].astype(F32), src[:, start : start + CHUNK])
             dst[:, start : start + size] = whole[:, :size].astype(BF16)
 
-    def lanes_of(first, t):
-        return pl.ds(pl.multiple_of(first * MID + t * 128, 128), 128)
-
     flat = (owners * rows_each, 128)
     for t in range(PARTS):
         from_all_owners(lambda count: stage_of(half_buf, t, count, as_sem, ar_sem).wait_recv())
@@ -542,7 +542,7 @@
     for g in range(CHUNKS):
         lead_row(g).wait_send()
         trail_row(g).wait_send()
-    for copy in lead + trail + (swap,):
+    for copy in lead + trail + tuple(swaps):
         copy.wait_send()
     for t in range(PARTS):
         back(t).wait_send()
@@ -592,7 +592,7 @@
     dma = pltpu.SemaphoreType.DMA
     row_halo = pltpu.VMEM((CHUNKS, 16, HALF), BF16)
     col_halo = pltpu.VMEM((16, EDGE), BF16)
-    half = (owners * rows_each, MID)
+    half = (PARTS, owners * rows_each, 128)
     stripe = (rows_each, 128)
     halves = (PARTS, owners) + stripe
     parts = pl.pallas_call(
@@ -623,8 +623,8 @@
             pltpu.VMEM(halves, BF16), pltpu.VMEM((PARTS, n_col) + stripe, BF16),
             pltpu.VMEM((PARTS,) + stripe, BF16), pltpu.VMEM((PARTS, n_row // 2) + stripe, BF16),
             pltpu.VMEM(halves, BF16), pltpu.VMEM(halves, BF16),
-            dma((9,)), dma((2 * CHUNKS + 4,)), dma((2 * CHUNKS + 4,)), dma((1 + PARTS,)),
-            dma((1 + PARTS,)), dma((PARTS,)), dma((PARTS,)), dma((PARTS,)), dma((PARTS,)),
+            dma((9,)), dma((2 * CHUNKS + 4,)), dma((2 * CHUNKS + 4,)), dma((2 * PARTS,)),
+            dma((2 * PARTS,)), dma((PARTS,)), dma((PARTS,)), dma((PARTS,)), dma((PARTS,)),
             dma((PARTS,)), dma((PARTS,)),
             pltpu.SemaphoreType.REGULAR((4,)), pltpu.SemaphoreType.REGULAR((4,)),
             pltpu.SemaphoreType.REGULAR,

time: 57.1 us -> 56.7 us (level)
  no operation moved by 1% of the time
where the time goes in v9:
time: 56.7 us; the launch traced here: 56.4 us
  Pallas kernels  55.8 us (98%)
  between operations  0.65 us (1%)
    pallas_call x1, Pallas kernels, shards(): pl.pallas_call(functools.partial(block_kernel, n_row, n_col, spp, factor)...  53.4 us
    pallas_call x1, Pallas kernels, shards(): pl.pallas_call(finish_kernel, out_shape=outs, in_specs=[vmem] * 3, out_sp...  2.34 us

profile of v9, /device:TPU:1, one launch (start us, length us, event | category | flops | bytes accessed | tf_op | source)
XLA Modules:
  0.0 56.4 jit_solution(17935327654382686470)
XLA Ops:
  0.6 53.4 %shard_map.160 = (bf16[8,12288]{1,0:T(8,128)(2,1)}, bf16[8,12288]{1,0:T(8,128)(2,1)}, f32[208,768]{1,0:T(8,128)}) custom-call(bf16[8,12288]{1,0:T(8,128)(2,1)} %refs_0_.1, bf16[8,12288]{1,0:T(8,128)(2,1)} %refs_1_.1, bf16[192,576]{1,0:T(8,128)(2,1)} %refs_2_.1, f32[576]{0:T(1024)} %refs_3_.1, bf16[192,192]{1,0:T(8,128)(2,1)} %refs_4_.1, f32[192]{0:T(256)} %refs_5_.1, ...), custom_call_target="tpu_custom_call" | custom-call | tf_op jit(solution)/shard_map/pallas_call | solution.py:598
  54.1 2.3 %shard_map.161 = (bf16[8,12288]{1,0:T(8,128)(2,1)}, bf16[8,12288]{1,0:T(8,128)(2,1)}, f32[192,576]{1,0:T(8,128)}, f32[576]{0:T(1024)}, f32[192,192]{1,0:T(8,128)...) custom-call(bf16[8,12288]{1,0:T(8,128)(2,1)} %get-tuple-element.12.res, ...), custom_call_target="tpu_custom_call" | custom-call | tf_op jit(solution)/shard_map/pallas_call | solution.py:639
